TPU v7x, 512 devices: a whole 4x4x16 slice. The times are simulated.
512 devices in a mesh: seq: 16 (over y, z_lo), batch: 32 (over z_hi, x, core).
Axes of the slice: x: 4, y: 4, z: 16 (z_hi: 4, z_lo: 4; z = z_hi * 4 + z_lo), core: 2. Of those that a mesh axis runs over, the one named last changes fastest.
Arguments:
- history: bfloat16 [32, 16384, 256], P('batch', 'seq'), may hold values from -36 to 36
- cotangent: bfloat16 [32, 16384, 256], P('batch', 'seq'), may hold values from -6 to 6
- filter_weight: bfloat16 [2, 128, 128, 256], P(None, 'seq', 'batch'), may hold values from -4 to 4
- gain_first: float32 [256], replicated, may hold values from 0.1 to 1.9
- bias_first: float32 [256], replicated, may hold values from -3 to 3
- w_in: bfloat16 [256, 512], replicated, may hold values from -0.375 to 0.375
- w_out: bfloat16 [512, 256], replicated, may hold values from -0.25 to 0.25
- gain_second: float32 [256], replicated, may hold values from 0.1 to 1.9
Outputs:
- history_grad: bfloat16 [32, 16384, 256], P('batch', 'seq')
- filter_grad: float32 [2, 128, 128, 256], P(None, 'seq', 'batch')
All inputs are finite; a program needn't handle non-finite values.
Results may differ from a plain program's by a relative error of at most 0.025.
Values may be sent and summed in bfloat16 or wider, within the bound.
A program may use at most 64 MiB of HBM per device.

v0:
```python
import math

import jax
import jax.numpy as jnp
from jax import lax
from jax.sharding import PartitionSpec as P

F1 = 128
F2 = 128


epsilon = 1e-05
inv_root_two = 1.0 / math.sqrt(2.0)
inv_root_tau = 1.0 / math.sqrt(2.0 * math.pi)


def dft_table(length):
    positions = jnp.arange(length, dtype=jnp.int32)
    phases = (positions[:, None] * positions[None, :] % length).astype(jnp.float32) * (
        2.0 * math.pi / length
    )
    return (jnp.cos(phases).astype(jnp.bfloat16), jnp.sin(phases).astype(jnp.bfloat16))


def twiddle(row_index, col_index, modulus):
    phases = (row_index[:, None] * col_index[None, :] % modulus).astype(jnp.float32) * (
        2.0 * math.pi / modulus
    )
    return (jnp.cos(phases)[:, :, None], jnp.sin(phases)[:, :, None])


def make_tables(cos_one, sin_one, cos_two, sin_two):
    outer_fwd = jnp.concatenate([cos_one, -sin_one], axis=0)
    inner_fwd = jnp.stack([jnp.stack([cos_two, sin_two]), jnp.stack([-sin_two, cos_two])])
    inner_inv = jnp.stack([jnp.stack([cos_two, -sin_two]), jnp.stack([sin_two, cos_two])])
    outer_inv = jnp.stack([cos_one, -sin_one])
    return (outer_fwd, inner_fwd, inner_inv, outer_inv)


def first_forward(values, outer_fwd, tw_cos, tw_sin):
    length = outer_fwd.shape[1]
    both = jnp.einsum("ka,uabd->ukbd", outer_fwd, values, preferred_element_type=jnp.float32)
    real_part, imag_part = (both[:, :length], both[:, length:])
    return jnp.stack(
        [real_part * tw_cos + imag_part * tw_sin, imag_part * tw_cos - real_part * tw_sin]
    ).astype(jnp.bfloat16)


def second_forward(complex_pair, inner_fwd):
    return jnp.einsum(
        "jiqb,iupbd->jupqd", inner_fwd, complex_pair, preferred_element_type=jnp.float32
    ).astype(jnp.bfloat16)


def first_inverse(complex_pair, inner_inv, tw_cos, tw_sin):
    both = jnp.einsum(
        "jiqb,iupqd->jupbd", inner_inv, complex_pair, preferred_element_type=jnp.float32
    )
    real_part, imag_part = (both[0], both[1])
    return jnp.stack(
        [real_part * tw_cos - imag_part * tw_sin, imag_part * tw_cos + real_part * tw_sin]
    ).astype(jnp.bfloat16)


def second_inverse(complex_pair, outer_inv, factor):
    return (
        jnp.einsum("ipa,iupbd->uabd", outer_inv, complex_pair, preferred_element_type=jnp.float32)
        * factor
    )


def filter_apply(spectrum, filter_full):
    spec_re, spec_im = (spectrum[0].astype(jnp.float32), spectrum[1].astype(jnp.float32))
    filt_re, filt_im = (filter_full[0].astype(jnp.float32), filter_full[1].astype(jnp.float32))
    return jnp.stack(
        [spec_re * filt_re - spec_im * filt_im, spec_re * filt_im + spec_im * filt_re]
    ).astype(jnp.bfloat16)


def filter_back(slope_spec, filter_full):
    slope_re, slope_im = (slope_spec[0].astype(jnp.float32), slope_spec[1].astype(jnp.float32))
    filt_re, filt_im = (filter_full[0].astype(jnp.float32), filter_full[1].astype(jnp.float32))
    return jnp.stack(
        [filt_re * slope_re + filt_im * slope_im, filt_re * slope_im - filt_im * slope_re]
    ).astype(jnp.bfloat16)


def filter_term(spectrum, slope_spec, factor):
    spec_re, spec_im = (spectrum[0].astype(jnp.float32), spectrum[1].astype(jnp.float32))
    slope_re, slope_im = (slope_spec[0].astype(jnp.float32), slope_spec[1].astype(jnp.float32))
    term_re = jnp.sum((spec_re * slope_re + spec_im * slope_im) * factor, axis=0)
    term_im = jnp.sum((spec_re * slope_im - spec_im * slope_re) * factor, axis=0)
    return jnp.stack([term_re, term_im])


def local_pass(
    mixed_rows, history_rows, cot_rows, gain_first, bias_first, w_in, w_out, gain_second
):
    summed = mixed_rows.astype(jnp.float32) + history_rows.astype(jnp.float32)
    center_one = summed - jnp.mean(summed, axis=-1, keepdims=True)
    inv_one = lax.rsqrt(jnp.mean(center_one * center_one, axis=-1, keepdims=True) + epsilon)
    norm_one = center_one * inv_one
    hidden = (norm_one * gain_first + bias_first).astype(jnp.bfloat16)
    preact = jnp.dot(hidden, w_in, preferred_element_type=jnp.float32)
    cumul = 0.5 * (1.0 + lax.erf(preact * inv_root_two))
    activation = (preact * cumul).astype(jnp.bfloat16)
    output_sum = jnp.dot(activation, w_out, preferred_element_type=jnp.float32) + hidden.astype(
        jnp.float32
    )
    center_two = output_sum - jnp.mean(output_sum, axis=-1, keepdims=True)
    inv_two = lax.rsqrt(jnp.mean(center_two * center_two, axis=-1, keepdims=True) + epsilon)
    norm_two = center_two * inv_two
    grad_norm = cot_rows.astype(jnp.float32) * gain_second
    grad_sum = inv_two * (
        grad_norm
        - jnp.mean(grad_norm, axis=-1, keepdims=True)
        - norm_two * jnp.mean(grad_norm * norm_two, axis=-1, keepdims=True)
    )
    grad_act = jnp.dot(grad_sum.astype(jnp.bfloat16), w_out.T, preferred_element_type=jnp.float32)
    density = jnp.exp(-0.5 * preact * preact) * inv_root_tau
    grad_pre = (grad_act * (cumul + preact * density)).astype(jnp.bfloat16)
    grad_hidden = jnp.dot(grad_pre, w_in.T, preferred_element_type=jnp.float32) + grad_sum
    grad_scaled = grad_hidden * gain_first
    grad_input = inv_one * (
        grad_scaled
        - jnp.mean(grad_scaled, axis=-1, keepdims=True)
        - norm_one * jnp.mean(grad_scaled * norm_one, axis=-1, keepdims=True)
    )
    return (grad_input, grad_input.astype(jnp.bfloat16))


def local(history, cotangent, filter_weight, gain_first, bias_first, w_in, w_out, gain_second):
    user_count, row_count, features = history.shape
    seq_count = lax.axis_size("seq")
    seq_rank = lax.axis_index("seq")
    slab_first = F1 // seq_count
    slab_second = F2 // seq_count
    cos_one, sin_one = dft_table(F1)
    cos_two, sin_two = dft_table(F2)
    outer_fwd, inner_fwd, inner_inv, outer_inv = make_tables(cos_one, sin_one, cos_two, sin_two)
    inv_length = 1.0 / (F1 * F2)
    weights = (gain_first, bias_first, w_in, w_out, gain_second)
    filter_full = lax.all_gather(filter_weight, "batch", axis=2, tiled=True)
    blocks = history.reshape(user_count, slab_first, F2, features)
    second_index = seq_rank * slab_second + jnp.arange(slab_second, dtype=jnp.int32)
    first_index = seq_rank * slab_first + jnp.arange(slab_first, dtype=jnp.int32)
    fwd_cos, fwd_sin = twiddle(jnp.arange(F1, dtype=jnp.int32), second_index, F1 * F2)
    inv_cos, inv_sin = twiddle(first_index, jnp.arange(F2, dtype=jnp.int32), F1 * F2)

    def second_section(block_part):
        return second_forward(block_part, inner_fwd)

    def finish(block_part):
        return second_inverse(block_part, outer_inv, inv_length)

    def to_spectrum(values):
        half_done = first_forward(values, outer_fwd, fwd_cos, fwd_sin)
        return second_section(
            lax.all_to_all(half_done, "seq", split_axis=2, concat_axis=3, tiled=True)
        )

    def to_field(complex_pair):
        half_done = first_inverse(complex_pair, inner_inv, inv_cos, inv_sin)
        return finish(lax.all_to_all(half_done, "seq", split_axis=3, concat_axis=2, tiled=True))

    spread = lax.all_to_all(blocks, "seq", split_axis=2, concat_axis=1, tiled=True)
    spectrum = to_spectrum(spread)
    seq_mix = to_field(filter_apply(spectrum, filter_full)).astype(jnp.bfloat16)
    seq_home = lax.all_to_all(seq_mix, "seq", split_axis=1, concat_axis=2, tiled=True)
    grad_input, slope = local_pass(
        seq_home.reshape(-1, features),
        history.reshape(-1, features),
        cotangent.reshape(-1, features),
        *weights
    )
    slope_spread = lax.all_to_all(
        slope.reshape(user_count, slab_first, F2, features),
        "seq",
        split_axis=2,
        concat_axis=1,
        tiled=True,
    )
    slope_spec = to_spectrum(slope_spread)
    back_field = to_field(filter_back(slope_spec, filter_full)).astype(jnp.bfloat16)
    back_home = lax.all_to_all(back_field, "seq", split_axis=1, concat_axis=2, tiled=True)
    history_grad = (grad_input + back_home.reshape(-1, features).astype(jnp.float32)).astype(
        jnp.bfloat16
    )
    history_grad = history_grad.reshape(user_count, row_count, features)
    partial_value = filter_term(spectrum, slope_spec, inv_length)
    filter_grad = lax.psum_scatter(
        partial_value.astype(jnp.bfloat16), "batch", scatter_dimension=2, tiled=True
    ).astype(jnp.float32)
    return (history_grad, filter_grad)


def solution(mesh):
    placed = (
        P("batch", "seq", None),
        P("batch", "seq", None),
        P(None, "seq", "batch", None),
        P(),
        P(),
        P(),
        P(),
        P(),
    )
    return jax.shard_map(
        local,
        mesh=mesh,
        in_specs=placed,
        out_specs=(P("batch", "seq", None), P(None, "seq", "batch", None)),
        check_vma=False,
    )
```

profile of v0, /device:TPU:25, one launch (start us, length us, event | category | flops | bytes accessed | tf_op | source)
XLA Modules:
  0.0 422.6 jit_solution(4154025189408776034)
XLA Ops:
  7.2 2.2 copy.155
  9.3 8.2 %all-to-all-start = ((bf16[1,8,128,256]{3,1,0,2:T(8,128)(2,1)}), bf16[1,8,128,256]{3,1,0,2:T(8,128)(2,1)S(1)}, u32[]{:S(2)}, u32[]{:S(2)}) async-start(bf16[1,8,128,256]{3,1,0,2:T(8,128)(2,1)} %copy.155), calls=%async_computation | async-start | bytes 1048576 | tf_op jit(solution)/shard_map/all_to_all | solution.py:166
  18.2 13.0 %all-to-all-done = bf16[1,8,128,256]{3,1,0,2:T(8,128)(2,1)S(1)} async-done(((bf16[1,8,128,256]{3,1,0,2:T(8,128)(2,1)}), bf16[1,8,128,256]{3,1,0,2:T(8,128)(2,1)S(1)}, u32[]{:S(2)}, u32[]{:S(2)}) %all-to-all-start) | async-done | bytes 524320 | tf_op jit(solution)/shard_map/all_to_all | solution.py:166
  32.4 1.6 copy.158
  34.0 5.6 %all-to-all-start.1 = ((bf16[2,1,128,8,256]{4,3,1,0,2:T(8,128)(2,1)}), bf16[2,1,128,8,256]{4,3,1,0,2:T(8,128)(2,1)S(1)}, u32[]{:S(2)}, u32[]{:S(2)}) async-start(bf16[2,1,128,8,256]{4,3,1,0,2:T(8,128)(2,1)} %copy.158), calls=%async_computation.1 | async-start | bytes 2097152 | tf_op jit(solution)/shard_map/all_to_all | solution.py:159
  39.6 0.6 copy.163
  40.9 0.7 fusion.90
  41.7 77.5 %all-gather.2.cloned.1.call-done = bf16[2,8,128,256]{3,1,0,2:T(8,128)(2,1)} async-done(((bf16[2,8,4,256]{3,1,0,2:T(8,128)(2,1)}), bf16[2,8,128,256]{3,1,0,2:T(8,128)(2,1)}) %all-gather.2.cloned.1.call-update) | async-done | bytes 1048592 | tf_op jit(solution)/shard_map/all_gather | solution.py:143
  119.2 1.3 fusion.120
  121.4 1.4 fusion.6
  124.6 1.0 copy.167
  125.6 29.5 %all_to_all.108 = bf16[2,1,8,128,256]{4,0,2,1,3:T(2,128)(2,1)S(1)} all-to-all(bf16[2,1,8,128,256]{4,0,2,1,3:T(2,128)(2,1)S(1)} %copy.167), channel_id=1, replica_groups=mesh['seq'=16,'batch'=32] {'seq'}, dimensions={3} | all-to-all | bytes 2097152 | tf_op jit(solution)/shard_map/all_to_all | solution.py:164
  156.4 1.2 copy.171
  157.6 6.1 %all-to-all-start.3 = ((bf16[1,128,8,256]{3,2,0,1:T(8,128)(2,1)}), bf16[1,128,8,256]{3,2,0,1:T(8,128)(2,1)S(1)}, u32[]{:S(2)}, u32[]{:S(2)}) async-start(bf16[1,128,8,256]{3,2,0,1:T(8,128)(2,1)} %copy.171), calls=%async_computation.3 | async-start | bytes 1048576 | tf_op jit(solution)/shard_map/all_to_all | solution.py:169
  163.8 13.6 %all-to-all-done.3 = bf16[1,128,8,256]{3,2,0,1:T(8,128)(2,1)S(1)} async-done(((bf16[1,128,8,256]{3,2,0,1:T(8,128)(2,1)}), bf16[1,128,8,256]{3,2,0,1:T(8,128)(2,1)S(1)}, u32[]{:S(2)}, u32[]{:S(2)}) %all-to-all-start.3) | async-done | bytes 524320 | tf_op jit(solution)/shard_map/all_to_all | solution.py:169
  177.4 0.8 fusion.68
  178.2 1.5 copy.174
  179.7 1.4 broadcast_multiply_fusion
  181.1 1.5 copy.179
  182.6 1.5 copy.175
  184.0 1.1 convert_bitcast_fusion.1
  185.1 1.5 div.28
  186.6 1.9 multiply_reduce_fusion.2
  188.5 0.9 copy.176
  189.7 1.3 copy.178
  192.3 0.7 fusion.121
  193.0 0.6 copy-done.1
  194.1 0.6 fusion.32
  194.7 0.6 broadcast_multiply_fusion.4
  195.3 0.6 broadcast_multiply_fusion.3
  195.9 5.4 %fusion.119 = (f32[1024]{0:T(1024)}, f32[1024]{0:T(1024)}, f32[1024,256]{1,0:T(8,128)}) fusion(f32[1024,256]{1,0:T(8,128)S(1)} %fusion.39, f32[256]{0:T(256)} %param.11, f32[1024]{0:T(1024)} %broadcast_multiply_fusion.3, f32[1024,256]{1,0:T(8,128)S(1)} %get-tuple-element.47, f32[1024]{0:T(1024)} %copy-done.23, f32[1024]{0:T(1024)} %broadcast_multiply_fusion.4, ...), kind=kOutput, calls=%fused_computation.203 | convolution fusion | flops 547878912 | bytes 6318080 | tf_op jit(solution)/shard_map/dot_general | solution.py:122
  201.3 0.7 broadcast_multiply_fusion.2
  202.0 0.7 broadcast_multiply_fusion.1
  202.7 1.7 fusion.118
  204.7 19.0 %all_to_all.109 = bf16[1,8,128,256]{3,1,0,2:T(8,128)(2,1)S(1)} all-to-all(bf16[1,8,128,256]{3,1,0,2:T(8,128)(2,1)S(1)} %copy.180), channel_id=1, replica_groups=mesh['seq'=16,'batch'=32] {'seq'}, dimensions={2} | all-to-all | bytes 1048576 | tf_op jit(solution)/shard_map/all_to_all | solution.py:176
  224.8 0.6 copy.185
  225.4 30.3 %all_to_all.110 = bf16[2,1,128,8,256]{4,3,1,0,2:T(8,128)(2,1)S(1)} all-to-all(bf16[2,1,128,8,256]{4,3,1,0,2:T(8,128)(2,1)S(1)} %copy.185), channel_id=1, replica_groups=mesh['seq'=16,'batch'=32] {'seq'}, dimensions={2} | all-to-all | bytes 2097152 | tf_op jit(solution)/shard_map/all_to_all | solution.py:159
  256.3 0.6 copy-done.4
  256.9 1.8 fusion.25
  259.7 1.0 copy.191
  260.7 30.1 %all_to_all.111 = bf16[2,1,8,128,256]{4,0,2,1,3:T(2,128)(2,1)S(1)} all-to-all(bf16[2,1,8,128,256]{4,0,2,1,3:T(2,128)(2,1)S(1)} %copy.191), channel_id=1, replica_groups=mesh['seq'=16,'batch'=32] {'seq'}, dimensions={3} | all-to-all | bytes 2097152 | tf_op jit(solution)/shard_map/all_to_all | solution.py:164
  292.1 1.2 copy.195
  293.3 5.5 %all-to-all-start.7 = ((bf16[1,128,8,256]{3,2,0,1:T(8,128)(2,1)}), bf16[1,128,8,256]{3,2,0,1:T(8,128)(2,1)S(1)}, u32[]{:S(2)}, u32[]{:S(2)}) async-start(bf16[1,128,8,256]{3,2,0,1:T(8,128)(2,1)} %copy.195), calls=%async_computation.7 | async-start | bytes 1048576 | tf_op jit(solution)/shard_map/all_to_all | solution.py:185
  298.9 1.1 pad_maximum_fusion.4
  300.0 1.7 copy.198
  301.8 111.0 %reduce-scatter.2.cloned.1.call-done = bf16[2,8,4,256]{3,1,0,2:T(8,128)(2,1)} async-done(((bf16[2,8,128,256]{3,1,0,2:T(8,128)(2,1)}), bf16[2,8,4,256]{3,1,0,2:T(8,128)(2,1)}) %reduce-scatter.2.cloned.1.call-update) | async-done | bytes 32784 | tf_op jit(solution)/shard_map/reduce_scatter | solution.py:191
  412.8 1.4 copy.199
  414.5 1.3 fusion.36
  (118 shorter events, 13.0 us)
Async XLA Ops:
  7.2 184.2 %copy-start = (bf16[256,512]{1,0:T(8,128)(2,1)S(1)}, bf16[256,512]{1,0:T(8,128)(2,1)}, u32[]{:S(2)}) copy-start(bf16[256,512]{1,0:T(8,128)(2,1)} %param.13) | copy-start | bytes 786436
  9.3 21.9 %all-to-all-start = ((bf16[1,8,128,256]{3,1,0,2:T(8,128)(2,1)}), bf16[1,8,128,256]{3,1,0,2:T(8,128)(2,1)S(1)}, u32[]{:S(2)}, u32[]{:S(2)}) async-start(bf16[1,8,128,256]{3,1,0,2:T(8,128)(2,1)} %copy.155), calls=%async_computation | async-start | bytes 1048576 | tf_op jit(solution)/shard_map/all_to_all | solution.py:166
  17.8 14.4 %copy-start.8 = (bf16[128,128]{1,0:T(8,128)(2,1)}, bf16[128,128]{1,0:T(8,128)(2,1)S(1)}, u32[]{:S(2)}) copy-start(bf16[128,128]{1,0:T(8,128)(2,1)S(1)} %fusion.89) | copy-start | bytes 98308
  18.1 14.2 %copy-start.10 = (bf16[128,128]{1,0:T(8,128)(2,1)}, bf16[128,128]{1,0:T(8,128)(2,1)S(1)}, u32[]{:S(2)}) copy-start(bf16[128,128]{1,0:T(8,128)(2,1)S(1)} %cosine_convert_fusion.1) | copy-start | bytes 98308
  32.4 7.2 %copy-start.28 = (bf16[2,8,4,256]{3,2,1,0:T(4,128)(2,1)S(1)}, bf16[2,8,4,256]{3,2,1,0:T(4,128)(2,1)}, u32[]{:S(2)}) copy-start(bf16[2,8,4,256]{3,2,1,0:T(4,128)(2,1)} %param.10) | copy-start | bytes 98308
  34.0 87.4 %all-to-all-start.1 = ((bf16[2,1,128,8,256]{4,3,1,0,2:T(8,128)(2,1)}), bf16[2,1,128,8,256]{4,3,1,0,2:T(8,128)(2,1)S(1)}, u32[]{:S(2)}, u32[]{:S(2)}) async-start(bf16[2,1,128,8,256]{4,3,1,0,2:T(8,128)(2,1)} %copy.158), calls=%async_computation.1 | async-start | bytes 2097152 | tf_op jit(solution)/shard_map/all_to_all | solution.py:159
  39.6 79.6 %all-gather.2.cloned.1.call-start = ((), (), s32[]{:S(2)}) async-start(), calls=%async_computation.9 | async-start | bytes 1081344 | tf_op jit(solution)/shard_map/all_gather | solution.py:143
  40.6 1.1 copy-start.15
  40.9 0.8 copy-start.18
  41.7 82.5 %copy-start.21 = (f32[8,128]{1,0:T(8,128)}, f32[8,128]{1,0:T(8,128)S(1)}, u32[]{:S(2)}) copy-start(f32[8,128]{1,0:T(8,128)S(1)} %get-tuple-element.43) | copy-start | bytes 12292
  122.8 1.0 copy-start.3
  155.1 0.8 copy-start.16
  155.1 0.8 copy-start.19
  155.6 8.1 %copy-start.2 = (bf16[1,1024,256]{2,1,0:T(8,128)(2,1)S(1)}, bf16[1,1024,256]{2,1,0:T(8,128)(2,1)}, u32[]{:S(2)}) copy-start(bf16[1,1024,256]{2,1,0:T(8,128)(2,1)} %param.8) | copy-start | bytes 1572868
  157.6 19.8 %all-to-all-start.3 = ((bf16[1,128,8,256]{3,2,0,1:T(8,128)(2,1)}), bf16[1,128,8,256]{3,2,0,1:T(8,128)(2,1)S(1)}, u32[]{:S(2)}, u32[]{:S(2)}) async-start(bf16[1,128,8,256]{3,2,0,1:T(8,128)(2,1)} %copy.171), calls=%async_computation.3 | async-start | bytes 1048576 | tf_op jit(solution)/shard_map/all_to_all | solution.py:169
  188.5 2.5 copy-start.29
  189.6 1.7 copy-start.31
  189.6 1.7 copy-start.32
  191.4 1.0 copy-start.12
  192.3 1.3 copy-start.1
  192.3 1.7 copy-start.7
  192.3 1.7 copy-start.33
  193.7 1.0 copy-start.23
  194.1 0.7 copy-start.30
  202.0 2.4 copy-start.24
  202.7 1.7 copy-start.26
  204.4 19.5 %copy-start.9 = (bf16[128,128]{1,0:T(8,128)(2,1)S(1)}, bf16[128,128]{1,0:T(8,128)(2,1)}, u32[]{:S(2)}) copy-start(bf16[128,128]{1,0:T(8,128)(2,1)} %copy-done.8) | copy-start | bytes 98308
  204.4 19.5 %copy-start.11 = (bf16[128,128]{1,0:T(8,128)(2,1)S(1)}, bf16[128,128]{1,0:T(8,128)(2,1)}, u32[]{:S(2)}) copy-start(bf16[128,128]{1,0:T(8,128)(2,1)} %copy-done.10) | copy-start | bytes 98308
  225.4 30.4 %copy-start.13 = (bf16[1,2,128,128]{3,2,1,0:T(8,128)(2,1)S(1)}, bf16[1,2,128,128]{3,2,1,0:T(8,128)(2,1)}, u32[]{:S(2)}) copy-start(bf16[1,2,128,128]{3,2,1,0:T(8,128)(2,1)} %get-tuple-element.37) | copy-start | bytes 196612
  225.4 30.4 %copy-start.14 = (bf16[1,2,128,128]{3,2,1,0:T(8,128)(2,1)S(1)}, bf16[1,2,128,128]{3,2,1,0:T(8,128)(2,1)}, u32[]{:S(2)}) copy-start(bf16[1,2,128,128]{3,2,1,0:T(8,128)(2,1)} %get-tuple-element.40) | copy-start | bytes 196612
  255.7 1.2 copy-start.4
  258.7 0.7 copy-start.22
  290.8 0.8 copy-start.17
  290.8 0.8 copy-start.20
  291.3 7.6 %copy-start.6 = (bf16[1,8,128,256]{2,3,1,0:T(8,128)(2,1)S(1)}, bf16[1,8,128,256]{2,3,1,0:T(8,128)(2,1)}, u32[]{:S(2)}) copy-start(bf16[1,8,128,256]{2,3,1,0:T(8,128)(2,1)} %get-tuple-element.26) | copy-start | bytes 1572868
  293.3 120.9 %all-to-all-start.7 = ((bf16[1,128,8,256]{3,2,0,1:T(8,128)(2,1)}), bf16[1,128,8,256]{3,2,0,1:T(8,128)(2,1)S(1)}, u32[]{:S(2)}, u32[]{:S(2)}) async-start(bf16[1,128,8,256]{3,2,0,1:T(8,128)(2,1)} %copy.195), calls=%async_computation.7 | async-start | bytes 1048576 | tf_op jit(solution)/shard_map/all_to_all | solution.py:185
  298.8 114.0 %reduce-scatter.2.cloned.1.call-start = ((), (), s32[]{:S(2)}) async-start(), calls=%async_computation.10 | async-start | bytes 1081344 | tf_op jit(solution)/shard_map/reduce_scatter | solution.py:191
  301.8 112.7 %copy-start.5 = (f32[1024,256]{1,0:T(8,128)S(1)}, f32[1024,256]{1,0:T(8,128)}, u32[]{:S(2)}) copy-start(f32[1024,256]{1,0:T(8,128)} %get-tuple-element.48) | copy-start | bytes 3145732
  301.8 112.7 %copy-start.25 = (f32[1024]{0:T(1024)S(1)}, f32[1024]{0:T(1024)}, u32[]{:S(2)}) copy-start(f32[1024]{0:T(1024)} %copy-done.24) | copy-start | bytes 12292
  301.8 112.7 %copy-start.27 = (f32[1024]{0:T(1024)S(1)}, f32[1024]{0:T(1024)}, u32[]{:S(2)}) copy-start(f32[1024]{0:T(1024)} %copy-done.26) | copy-start | bytes 12292
Sparse Core Ops, SparseCore 0:
  44.1 75.0 all-gather.1
  304.0 108.7 reduce-scatter.1
where the time goes:
time: 426 us; the launch traced here: 423 us
  waiting for transfers between devices  215 us (50%)
  blocking collectives  109 us (26%)
  local copies, waits for them, and re-layouts  27.9 us (7%)
  starting transfers between devices  25.5 us (6%)
  other arithmetic  19.2 us (5%)
  between operations  14.7 us (3%)
  matrix products  11.3 us (3%)
    reduce_scatter x1, waiting for transfers between devices, local(): lax.psum_scatter(partial_value.astype(jnp.bfloat16), 'batch', scatter_dim...  111 us
    all_gather x1, waiting for transfers between devices, local(): filter_full = lax.all_gather(filter_weight, 'batch', axis=2, tiled=True)  77.5 us
    all_to_all x2, blocking collectives, to_field(): lax.all_to_all(half_done, 'seq', split_axis=3, concat_axis=2, tiled=True)  59.5 us
    all_to_all x1, blocking collectives, to_spectrum(): lax.all_to_all(half_done, 'seq', split_axis=2, concat_axis=3, tiled=True)  30.3 us
    all_to_all x1, blocking collectives, local(): lax.all_to_all(slope.reshape(user_count, slab_first, F2, features), 'seq'...  19 us
    all_to_all x1, waiting for transfers between devices, local(): lax.all_to_all(seq_mix, 'seq', split_axis=1, concat_axis=2, tiled=True)  13.6 us
    all_to_all x1, waiting for transfers between devices, local(): lax.all_to_all(blocks, 'seq', split_axis=2, concat_axis=1, tiled=True)  13 us
  transfers between devices with their start and end apart: 6, of which 4 were waited for; matrix products, arithmetic and copies ran while one was open for 2% of the time, Pallas kernels for 0%

commit v1 on v0

v1 whole, which is shorter than its diff:
```python
import functools
import math

import jax
import jax.numpy as jnp
import ml_dtypes
import numpy as np
from jax import lax
from jax.experimental import pallas as pl
from jax.experimental.pallas import tpu as pltpu
from jax.sharding import PartitionSpec as P

F1 = 128
F2 = 128
LINES = 64
CHUNK = 2

epsilon = 1e-05
inv_root_two = 1.0 / math.sqrt(2.0)
inv_root_tau = 1.0 / math.sqrt(2.0 * math.pi)
inv_length = 1.0 / (F1 * F2)


def host_tables():
    index = np.arange(F1)
    angle = 2.0 * np.pi * (index[:, None] * index[None, :] % F1) / F1
    cos, sin = np.cos(angle), np.sin(angle)
    outer_fwd = np.concatenate([cos[:LINES], -sin[:LINES]], axis=0)
    outer_inv = np.concatenate([cos[:LINES], -sin[:LINES]], axis=0).T
    inner_fwd = np.block([[cos, -sin], [sin, cos]])
    inner_inv = np.block([[cos, sin], [-sin, cos]])
    lines = np.arange(LINES + 1)
    phase = 2.0 * np.pi * (lines[:, None] * index[None, :]) / (F1 * F2)
    narrow = [t.astype(ml_dtypes.bfloat16) for t in (outer_fwd, outer_inv, inner_fwd, inner_inv)]
    twiddles = np.stack([np.cos(phase), np.sin(phase)]).astype(np.float32)
    return (*narrow, twiddles[:, :LINES], twiddles[:, LINES:])


def dot(a, b):
    return jnp.dot(a, b, preferred_element_type=jnp.float32)


def dot_nt(a, b):
    return lax.dot_general(a, b, (((1,), (1,)), ((), ())), preferred_element_type=jnp.float32)


def mean(x):
    return jnp.mean(x, axis=-1, keepdims=True)


def local_rows(mixed, history, cot, gain_first, bias_first, w_in, w_out, gain_second):
    summed = mixed + history.astype(jnp.float32)
    center_one = summed - mean(summed)
    inv_one = lax.rsqrt(mean(center_one * center_one) + epsilon)
    norm_one = center_one * inv_one
    hidden = (norm_one * gain_first + bias_first).astype(jnp.bfloat16)
    preact = dot(hidden, w_in)
    cumul = 0.5 * (1.0 + lax.erf(preact * inv_root_two))
    activation = (preact * cumul).astype(jnp.bfloat16)
    output_sum = dot(activation, w_out) + hidden.astype(jnp.float32)
    center_two = output_sum - mean(output_sum)
    inv_two = lax.rsqrt(mean(center_two * center_two) + epsilon)
    norm_two = center_two * inv_two
    grad_norm = cot.astype(jnp.float32) * gain_second
    grad_sum = inv_two * (grad_norm - mean(grad_norm) - norm_two * mean(grad_norm * norm_two))
    grad_act = dot_nt(grad_sum.astype(jnp.bfloat16), w_out)
    density = jnp.exp(-0.5 * preact * preact) * inv_root_tau
    grad_pre = (grad_act * (cumul + preact * density)).astype(jnp.bfloat16)
    grad_hidden = dot_nt(grad_pre, w_in) + grad_sum
    grad_scaled = grad_hidden * gain_first
    return inv_one * (grad_scaled - mean(grad_scaled) - norm_one * mean(grad_scaled * norm_one))


def kernel(
    seq,
    history,
    cotangent,
    filt,
    filt_mid,
    gain_first,
    bias_first,
    w_in,
    w_out,
    gain_second,
    outer_fwd,
    outer_inv,
    inner_fwd,
    inner_inv,
    twiddle,
    twiddle_mid,
    out,
    grad,
    grad_mid,
    send_in,
    send_out,
    recv_in,
    recv_out,
    spec,
    spec_mid,
    field,
    grad_rows,
    send_sem,
    recv_sem,
):
    me = lax.axis_index("seq")
    rows = F1 // seq
    feats = history.shape[1] // seq
    chunks = rows // CHUNK

    barrier = pltpu.get_barrier_semaphore()

    def greet(k, _):
        pl.semaphore_signal(
            barrier,
            inc=1,
            device_id={"seq": lax.rem(me + k, seq)},
            device_id_type=pl.DeviceIdType.MESH,
        )
        return 0

    lax.fori_loop(1, seq, greet, 0)
    pl.semaphore_wait(barrier, seq - 1)

    def exchange(src, dst, way, chunk):
        def one(k, _):
            peer = lax.rem(me + k, seq)
            pltpu.make_async_remote_copy(
                src_ref=src(peer),
                dst_ref=dst,
                send_sem=send_sem.at[way],
                recv_sem=recv_sem.at[way, chunk],
                device_id={"seq": peer},
                device_id_type=pl.DeviceIdType.MESH,
            ).start()
            return 0

        lax.fori_loop(1, seq, one, 0)

    def send_positions(x, way, chunk):
        for j in range(chunk * CHUNK, (chunk + 1) * CHUNK):
            block = x(j).T.reshape(seq, feats, F2)
            send_in[way, j] = block
        part = pl.ds(chunk * CHUNK, CHUNK)
        recv_in[way, me, part] = send_in[way, part, me]
        exchange(
            lambda peer: send_in.at[way, part, peer], recv_in.at[way, me, part], 2 * way, chunk
        )

    def send_features(way, chunk):
        part = pl.ds(chunk * CHUNK, CHUNK)
        recv_out[way, part, me] = send_out[way, me, part]
        exchange(
            lambda peer: send_out.at[way, peer, part], recv_out.at[way, part, me], 2 * way + 1, chunk
        )

    def wait_chunk(way, chunk):
        whole = send_in.at[0, pl.ds(0, CHUNK), pl.ds(0, seq - 1)]
        pltpu.make_async_copy(whole, whole, recv_sem.at[way, chunk]).wait()

    def transform(way, multiply, multiply_mid):
        tiles = recv_in[way].reshape(F1 // 2, 2, feats, F2)
        mid = jnp.sum(
            tiles[:, 0].astype(jnp.float32) - tiles[:, 1].astype(jnp.float32), axis=0
        )
        field[...] = recv_in[way].reshape(F1 * feats, F2).astype(jnp.float32)
        cos, sin = twiddle[0], twiddle[1]

        def pair(first):
            return [field[pl.ds(first + i, F1, stride=feats), :] for i in range(2)]

        def step(group, _):
            base = group * 4
            halves = []
            for sub in range(2):
                two = jnp.concatenate(pair(base + 2 * sub), axis=1).astype(jnp.bfloat16)
                both = dot(outer_fwd[...], two)
                for i in range(2):
                    real = both[:LINES, i * F2 : (i + 1) * F2]
                    imag = both[LINES:, i * F2 : (i + 1) * F2]
                    halves.append(
                        jnp.concatenate(
                            [real * cos + imag * sin, imag * cos - real * sin], axis=1
                        ).astype(jnp.bfloat16)
                    )
            spectrum = dot(jnp.concatenate(halves, axis=0), inner_fwd[...])
            where = pl.ds(pl.multiple_of(base * LINES, 4 * LINES), 4 * LINES)
            product = multiply(spectrum, where)
            half = dot(product, inner_inv[...])
            for sub in range(2):
                columns = []
                for i in range(2):
                    piece = half[(2 * sub + i) * LINES : (2 * sub + i + 1) * LINES]
                    real, imag = piece[:, :F2], piece[:, F2:]
                    columns.append(
                        jnp.concatenate(
                            [real * cos - imag * sin, imag * cos + real * sin], axis=0
                        ).astype(jnp.bfloat16)
                    )
                result = dot(outer_inv[...], jnp.concatenate(columns, axis=1)) * inv_length
                for i in range(2):
                    field[pl.ds(base + 2 * sub + i, F1, stride=feats), :] = result[
                        :, i * F2 : (i + 1) * F2
                    ]
            return 0

        lax.fori_loop(0, feats // 4, step, 0)

        cos_mid, sin_mid = twiddle_mid[0], twiddle_mid[1]
        half = jnp.concatenate([mid * cos_mid, -mid * sin_mid], axis=1).astype(jnp.bfloat16)
        product = multiply_mid(dot(half, inner_fwd[...]))
        half = dot(product, inner_inv[...])
        last = (half[:, :F2] * cos_mid - half[:, F2:] * sin_mid).astype(jnp.bfloat16)
        last = last.astype(jnp.float32) * inv_length
        both = field[...].reshape(F1 // 2, 2, feats, F2)
        sign = jnp.where(lax.broadcasted_iota(jnp.int32, both.shape, 1) == 0, 1.0, -1.0)
        both = both + sign * last[None, None]
        send_out[way] = both.astype(jnp.bfloat16).reshape(seq, rows, feats, F2)

    def split(z):
        return z[:, :F2].astype(jnp.float32), z[:, F2:].astype(jnp.float32)

    def times(z, f):
        zr, zi = split(z)
        fr, fi = split(f)
        return jnp.concatenate([zr * fr - zi * fi, zr * fi + zi * fr], axis=1).astype(jnp.bfloat16)

    def times_conj(z, f):
        zr, zi = split(z)
        fr, fi = split(f)
        return jnp.concatenate([fr * zr + fi * zi, fr * zi - fi * zr], axis=1)

    def filter_main(z, where):
        z = z.astype(jnp.bfloat16)
        spec[where, :] = z
        return times(z, filt[where, :])

    def filter_mid(z):
        z = z.astype(jnp.bfloat16)
        spec_mid[...] = z
        return times(z, filt_mid[...])

    def back_main(z, where):
        z = z.astype(jnp.bfloat16)
        grad[where, :] = (times_conj(z, spec[where, :]) * inv_length).astype(jnp.bfloat16)
        return times_conj(z, filt[where, :]).astype(jnp.bfloat16)

    def back_mid(z):
        z = z.astype(jnp.bfloat16)
        grad_mid[...] = (times_conj(z, spec_mid[...]) * inv_length).astype(jnp.bfloat16)
        return times_conj(z, filt_mid[...]).astype(jnp.bfloat16)

    for chunk in range(chunks):
        send_positions(lambda j: history[pl.ds(j * F2, F2), :], 0, chunk)
    for chunk in range(chunks):
        wait_chunk(0, chunk)
    transform(0, filter_main, filter_mid)
    for chunk in range(chunks):
        send_features(0, chunk)

    for chunk in range(chunks):
        wait_chunk(1, chunk)
        for j in range(chunk * CHUNK, (chunk + 1) * CHUNK):
            mixed = recv_out[0, j].reshape(seq * feats, F2).T.astype(jnp.float32)
            part = pl.ds(j * F2, F2)
            grad_rows[part, :] = local_rows(
                mixed,
                history[part, :],
                cotangent[part, :],
                gain_first[...],
                bias_first[...],
                w_in[...],
                w_out[...],
                gain_second[...],
            )
        send_positions(
            lambda j: grad_rows[pl.ds(j * F2, F2), :].astype(jnp.bfloat16), 1, chunk
        )

    for chunk in range(chunks):
        wait_chunk(2, chunk)
    transform(1, back_main, back_mid)
    for chunk in range(chunks):
        send_features(1, chunk)
    for chunk in range(chunks):
        wait_chunk(3, chunk)
        for j in range(chunk * CHUNK, (chunk + 1) * CHUNK):
            back = recv_out[1, j].reshape(seq * feats, F2).T.astype(jnp.float32)
            part = pl.ds(j * F2, F2)
            out[part, :] = (grad_rows[part, :] + back).astype(jnp.bfloat16)

    sent = send_in.at[0, :, pl.ds(0, seq - 1)]
    for way in range(4):
        pltpu.make_async_copy(sent, sent, send_sem.at[way]).wait()


def local(history, cotangent, filter_weight, gain_first, bias_first, w_in, w_out, gain_second):
    user_count, row_count, features = history.shape
    seq = lax.axis_size("seq")
    feats = features // seq
    rows = F1 // seq
    bf16, f32 = jnp.bfloat16, jnp.float32
    tables = [jnp.asarray(t) for t in host_tables()]

    full = lax.all_to_all(filter_weight, "seq", split_axis=3, concat_axis=1, tiled=True)
    full = lax.all_gather(full, "batch", axis=2, tiled=True)
    mirrored = jnp.flip(full[:, LINES:], axis=(1, 2)).astype(f32) * jnp.array(
        [1.0, -1.0], f32
    ).reshape(2, 1, 1, 1)
    main = full[:, :LINES].astype(f32) + jnp.pad(
        mirrored[:, : LINES - 1], ((0, 0), (1, 0), (0, 0), (0, 0))
    )
    filt = main.astype(bf16).transpose(3, 1, 0, 2).reshape(feats * LINES, 2 * F2)
    filt_mid = mirrored[:, LINES - 1].astype(bf16).transpose(2, 0, 1).reshape(feats, 2 * F2)

    vmem = pl.BlockSpec(memory_space=pltpu.VMEM)
    out, grad, grad_mid = pl.pallas_call(
        functools.partial(kernel, seq),
        out_shape=(
            jax.ShapeDtypeStruct((row_count, features), bf16),
            jax.ShapeDtypeStruct((feats * LINES, 2 * F2), bf16),
            jax.ShapeDtypeStruct((feats, 2 * F2), bf16),
        ),
        in_specs=[vmem] * 15,
        out_specs=(vmem,) * 3,
        scratch_shapes=[
            pltpu.VMEM((2, rows, seq, feats, F2), bf16),
            pltpu.VMEM((2, seq, rows, feats, F2), bf16),
            pltpu.VMEM((2, seq, rows, feats, F2), bf16),
            pltpu.VMEM((2, rows, seq, feats, F2), bf16),
            pltpu.VMEM((feats * LINES, 2 * F2), bf16),
            pltpu.VMEM((feats, 2 * F2), bf16),
            pltpu.VMEM((F1 * feats, F2), f32),
            pltpu.VMEM((row_count, features), f32),
            pltpu.SemaphoreType.DMA((4,)),
            pltpu.SemaphoreType.DMA((4, rows // CHUNK)),
        ],
        compiler_params=pltpu.CompilerParams(
            collective_id=0, has_side_effects=True, vmem_limit_bytes=48 * 2**20
        ),
    )(
        history.reshape(row_count, features),
        cotangent.reshape(row_count, features),
        filt,
        filt_mid,
        gain_first.reshape(1, features),
        bias_first.reshape(1, features),
        w_in,
        w_out,
        gain_second.reshape(1, features),
        *tables
    )
    half = jnp.concatenate(
        [
            grad.reshape(feats, LINES, 2, F2).transpose(2, 1, 3, 0),
            grad_mid.reshape(feats, 1, 2, F2).transpose(2, 1, 3, 0),
        ],
        axis=1,
    )
    sign = jnp.array([1.0, -1.0], bf16).reshape(2, 1, 1, 1)
    whole = jnp.concatenate([half, jnp.flip(half[:, 1:LINES], axis=(1, 2)) * sign], axis=1)
    part = lax.psum_scatter(whole, "batch", scatter_dimension=2, tiled=True)
    filter_grad = lax.all_to_all(part, "seq", split_axis=1, concat_axis=3, tiled=True)
    return (out.reshape(user_count, row_count, features), filter_grad.astype(f32))


def solution(mesh):
    placed = (
        P("batch", "seq", None),
        P("batch", "seq", None),
        P(None, "seq", "batch", None),
        P(),
        P(),
        P(),
        P(),
        P(),
    )
    return jax.shard_map(
        local,
        mesh=mesh,
        in_specs=placed,
        out_specs=(P("batch", "seq", None), P(None, "seq", "batch", None)),
        check_vma=False,
    )
```

time: 426 us -> 311 us (0.73)
  blocking collectives: 109 us -> 13.2 us
  Pallas kernels: 0 us -> 59.2 us
  waiting for transfers between devices: 215 us -> 188 us
  starting transfers between devices: 25.5 us -> 4.64 us
  other arithmetic: 19.2 us -> 2.45 us
  matrix products: 11.3 us -> 0 us
  local copies, waits for them, and re-layouts: 27.9 us -> 23.2 us
    all_to_all x4 -> x1, blocking collectives: 109 us -> 13.2 us  [local(): lax.all_to_all(filter_weight, 'seq', split_axis=3, concat_axis=1, tiled=T...]
    pallas_call x0 -> x1, Pallas kernels: none -> 59.2 us  [local(): pl.pallas_call(functools.partial(kernel, seq), out_shape=(jax.ShapeDtypeS...]
    all_to_all x4 -> x1, waiting for transfers between devices: 26.6 us -> 5.16 us  [local(): lax.all_to_all(part, 'seq', split_axis=1, concat_axis=3, tiled=True)]
    all_to_all x4 -> x1, starting transfers between devices: 25.4 us -> 4.56 us  [local(): lax.all_to_all(part, 'seq', split_axis=1, concat_axis=3, tiled=True)]
    dot_general x11 -> x0, matrix products: 11.3 us -> none  [the longest x1 5.37 us: local_pass(): jnp.dot(grad_pre, w_in.T, preferred_element_type=jnp.float32) + grad_sum]
    another operation x5 -> x0, local copies, waits for them, and re-layouts: 5.83 us -> none  [the longest x2 2.15 us: first_forward(): jnp.stack([real_part * tw_cos + imag_part * tw_sin, imag_part * tw_cos -...]
    another operation x12 -> x0, other arithmetic: 5.66 us -> none
    convert_element_type x7 -> x1, other arithmetic: 4.83 us -> 0.07 us  [local(): filter_grad.astype(f32)]
  transfers between devices with their start and end apart: 6 -> 3, of which waited for: 4 -> 3; matrix products, arithmetic and copies ran while one was open for 2% -> 0% of each run, Pallas kernels for 0% -> 0%
where the time goes in v1:
time: 311 us; the launch traced here: 305 us
  waiting for transfers between devices  188 us (60%)
  Pallas kernels  59.2 us (19%)
  local copies, waits for them, and re-layouts  23.2 us (7%)
  between operations  14.4 us (5%)
  blocking collectives  13.2 us (4%)
  starting transfers between devices  4.64 us (1%)
    reduce_scatter x1, waiting for transfers between devices, local(): part = lax.psum_scatter(whole, 'batch', scatter_dimension=2, tiled=True)  108 us
    all_gather x1, waiting for transfers between devices, local(): full = lax.all_gather(full, 'batch', axis=2, tiled=True)  75 us
    pallas_call x1, Pallas kernels, local(): pl.pallas_call(functools.partial(kernel, seq), out_shape=(jax.ShapeDtypeS...  59.2 us
    all_to_all x1, blocking collectives, local(): lax.all_to_all(filter_weight, 'seq', split_axis=3, concat_axis=1, tiled=T...  13.2 us
    unnamed x41, local copies, waits for them, and re-layouts  8.92 us
  transfers between devices with their start and end apart: 3, of which 3 were waited for; matrix products, arithmetic and copies ran while one was open for 0% of the time, Pallas kernels for 0%

profile of v1, /device:TPU:25, one launch (start us, length us, event | category | flops | bytes accessed | tf_op | source)
XLA Modules:
  0.0 304.9 jit_solution(2423992973951278825)
XLA Ops:
  7.2 0.0 all-gather.2.cloned.1.call-start
  7.2 1.2 copy.41
  8.4 0.5 reshape.55
  8.9 13.2 %all_to_all.27 = bf16[16,2,512]{2,1,0:T(2,128)(2,1)S(1)} all-to-all(bf16[16,2,512]{2,1,0:T(2,128)(2,1)S(1)} %reshape.55), channel_id=1, replica_groups=mesh['seq'=16,'batch'=32] {'seq'}, dimensions={0} | all-to-all | bytes 65536 | tf_op jit(solution)/shard_map/all_to_all | solution.py:304
  22.1 0.6 reshape.56
  22.7 0.4 copy.42
  23.1 0.7 copy.43
  23.9 0.0 all-gather.2.cloned.1.call-update
  23.9 0.0 reduce-scatter.2.cloned.1.call-start
  24.0 75.0 %all-gather.2.cloned.1.call-done = bf16[2,128,128,16]{1,3,0,2:T(8,128)(2,1)} async-done(((bf16[2,128,4,16]{1,3,0,2:T(8,128)(2,1)}), bf16[2,128,128,16]{1,3,0,2:T(8,128)(2,1)}) %all-gather.2.cloned.1.call-update) | async-done | bytes 1048592 | tf_op jit(solution)/shard_map/all_gather | solution.py:305
  98.9 2.0 fusion.2
  100.9 1.4 copy.53
  102.4 0.6 rev.8
  103.0 0.1 convert_multiply_fusion
  103.1 0.1 slice.23
  103.2 1.4 copy.52
  104.6 0.1 fusion
  104.8 0.0 copy-start.4
  104.8 0.0 copy-start.5
  104.8 0.0 copy-start.6
  104.9 0.5 copy.46
  105.5 0.1 copy.58
  105.6 0.2 copy-done
  105.8 0.2 copy-done.1
  106.0 0.1 copy-done.2
  106.0 0.1 copy-done.3
  106.1 0.0 copy-done.4
  106.1 0.0 copy-done.5
  106.2 59.2 %shard_map.167 = (bf16[1024,256]{1,0:T(8,128)(2,1)S(1)}, bf16[1024,256]{1,0:T(8,128)(2,1)S(1)}, bf16[16,256]{1,0:T(8,128)(2,1)S(1)}) custom-call(bf16[1024,256]{1,0:T(8,128)(2,1)S(1)} %bitcast.38, bf16[1024,256]{1,0:T(8,128)(2,1)S(1)} %bitcast.39, bf16[1024,256]{1,0:T(8,128)(2,1)S(1)} %bitcast.37, bf16[16,256]{1,0:T(8,128)(2,1)S(1)} %copy_bitcast_fusion.1.filt_mid, ...), custom_call_target="tpu_custom_call" | custom-call | tf_op jit(solution)/shard_map/pallas_call | solution.py:316
  165.5 0.1 reshape.51
  165.6 1.1 copy.48
  166.7 2.6 copy.49
  169.3 1.3 slice.25
  170.6 2.7 rev.9
  173.3 0.1 broadcast_multiply_fusion
  173.5 1.1 copy-done.13
  174.5 2.0 pad_maximum_fusion
  176.5 0.0 reduce-scatter.2.cloned.1.call-update
  176.5 107.7 %reduce-scatter.2.cloned.1.call-done = bf16[2,128,4,16]{1,3,0,2:T(8,128)(2,1)} async-done(((bf16[2,128,128,16]{1,3,0,2:T(8,128)(2,1)}), bf16[2,128,4,16]{1,3,0,2:T(8,128)(2,1)}) %reduce-scatter.2.cloned.1.call-update) | async-done | bytes 32784 | tf_op jit(solution)/shard_map/reduce_scatter | solution.py:361
  284.2 0.9 copy.50
  285.2 0.9 reshape.57
  286.1 4.6 %all-to-all-start.1 = ((bf16[16,2,512]{2,1,0:T(2,128)(2,1)}), bf16[16,2,512]{2,1,0:T(2,128)(2,1)S(1)}, u32[]{:S(2)}, u32[]{:S(2)}) async-start(bf16[16,2,512]{2,1,0:T(2,128)(2,1)} %reshape.57), calls=%async_computation.2 | async-start | bytes 65536 | tf_op jit(solution)/shard_map/all_to_all | solution.py:362
  290.6 5.2 %all-to-all-done.1 = bf16[16,2,512]{2,1,0:T(2,128)(2,1)S(1)} async-done(((bf16[16,2,512]{2,1,0:T(2,128)(2,1)}), bf16[16,2,512]{2,1,0:T(2,128)(2,1)S(1)}, u32[]{:S(2)}, u32[]{:S(2)}) %all-to-all-start.1) | async-done | bytes 32800 | tf_op jit(solution)/shard_map/all_to_all | solution.py:362
  295.8 0.2 reshape.58
  296.0 0.1 convert_bitcast_fusion
  296.1 0.3 copy.51
  296.4 0.9 reshape.53
  297.3 0.8 copy.60
  (24 shorter events, 0.1 us)
Async XLA Ops:
  7.2 91.8 %all-gather.2.cloned.1.call-start = ((), (), s32[]{:S(2)}) async-start(), calls=%async_computation.3 | async-start | bytes 1081344 | tf_op jit(solution)/shard_map/all_gather | solution.py:305
  23.9 260.3 %reduce-scatter.2.cloned.1.call-start = ((), (), s32[]{:S(2)}) async-start(), calls=%async_computation.4 | async-start | bytes 1081344 | tf_op jit(solution)/shard_map/reduce_scatter | solution.py:361
  100.9 2.0 copy-start.15
  104.8 1.0 copy-start
  104.8 1.2 copy-start.1
  104.8 1.2 copy-start.2
  104.8 1.3 copy-start.3
  104.8 1.3 copy-start.4
  104.8 1.4 copy-start.5
  104.8 1.4 copy-start.6
  104.8 1.3 copy-start.7
  104.9 1.3 copy-start.8
  104.9 1.3 copy-start.9
  104.9 1.3 copy-start.10
  104.9 1.3 copy-start.11
  104.9 1.3 copy-start.12
  170.6 2.7 copy-start.14
  173.3 1.2 copy-start.13
  286.1 9.7 %all-to-all-start.1 = ((bf16[16,2,512]{2,1,0:T(2,128)(2,1)}), bf16[16,2,512]{2,1,0:T(2,128)(2,1)S(1)}, u32[]{:S(2)}, u32[]{:S(2)}) async-start(bf16[16,2,512]{2,1,0:T(2,128)(2,1)} %reshape.57), calls=%async_computation.2 | async-start | bytes 65536 | tf_op jit(solution)/shard_map/all_to_all | solution.py:362
Sparse Core Ops, SparseCore 0:
  24.0 74.8 all-gather.1
  176.6 107.5 reduce-scatter.1

commit v2 on v1

--- a/solution.py
+++ b/solution.py
@@ -14,6 +14,7 @@
 F2 = 128
 LINES = 64
 CHUNK = 2
+ZS, XS, CORES = 4, 4, 2
 
 epsilon = 1e-05
 inv_root_two = 1.0 / math.sqrt(2.0)
@@ -33,7 +34,18 @@
     phase = 2.0 * np.pi * (lines[:, None] * index[None, :]) / (F1 * F2)
     narrow = [t.astype(ml_dtypes.bfloat16) for t in (outer_fwd, outer_inv, inner_fwd, inner_inv)]
     twiddles = np.stack([np.cos(phase), np.sin(phase)]).astype(np.float32)
-    return (*narrow, twiddles[:, :LINES], twiddles[:, LINES:])
+    return (*narrow, twiddles[:, :LINES], twiddles[:, LINES:], *permutations())
+
+
+def permutations():
+    spread = np.zeros((2, 2 * F2, 4 * F2), np.float32)
+    collect = np.zeros((2 * F2, 2 * F2), np.float32)
+    for part in range(2):
+        for q in range(F2):
+            for h in range(2):
+                spread[h, part * F2 + q, (q // 4) * 16 + h * 8 + part * 4 + q % 4] = 1.0
+            collect[(q // 4) * 8 + part * 4 + q % 4, part * F2 + q] = 1.0
+    return spread.astype(ml_dtypes.bfloat16), collect.astype(ml_dtypes.bfloat16)
 
 
 def dot(a, b):
@@ -42,6 +54,29 @@
 
 def dot_nt(a, b):
     return lax.dot_general(a, b, (((1,), (1,)), ((), ())), preferred_element_type=jnp.float32)
+
+
+def mirror_rows(x):
+    axis = x.ndim - 2
+    size = x.shape[axis]
+    row = lax.broadcasted_iota(jnp.int32, x.shape, axis)
+    for step in (1, 2):
+        up, down = pltpu.roll(x, step, axis), pltpu.roll(x, size - step, axis)
+        x = jnp.where((row & step) != 0, up, down)
+    return jnp.where((row & 4) != 0, -x, x)
+
+
+def block_transpose(tiles):
+    lane = lax.broadcasted_iota(jnp.int32, tiles[0].shape, 1) // 16
+    result = []
+    for to in range(8):
+        total = tiles[to]
+        for block in range(8):
+            if block != to:
+                moved = pltpu.roll(tiles[block], 16 * ((block - to) % 8), 1)
+                total = jnp.where(lane == block, moved, total)
+        result.append(total)
+    return result
 
 
 def mean(x):
@@ -73,10 +108,10 @@
 
 def kernel(
     seq,
+    batch,
     history,
     cotangent,
-    filt,
-    filt_mid,
+    filter_weight,
     gain_first,
     bias_first,
     w_in,
@@ -88,38 +123,271 @@
     inner_inv,
     twiddle,
     twiddle_mid,
+    spread,
+    collect,
     out,
-    grad,
-    grad_mid,
+    filter_grad,
     send_in,
     send_out,
     recv_in,
     recv_out,
     spec,
     spec_mid,
+    filt,
+    filt_mid,
     field,
+    grad_field,
+    grad_mid,
     grad_rows,
+    stage,
+    scatter_send,
+    scatter_recv,
+    gathered,
+    core_send,
+    core_recv,
+    x_send,
+    x_recv,
+    z_send,
+    z_recv,
+    return_send,
+    return_recv,
     send_sem,
     recv_sem,
+    side_send_sem,
+    side_recv_sem,
 ):
     me = lax.axis_index("seq")
+    mine = lax.axis_index("batch")
     rows = F1 // seq
     feats = history.shape[1] // seq
     chunks = rows // CHUNK
+    core = lax.rem(mine, CORES)
+    along_x = lax.rem(mine // CORES, XS)
+    along_z = mine // (CORES * XS)
+    opposite = batch - 1 - mine
+    low = me < seq // 2
+
+    def batch_index(z, x, c):
+        return (z * XS + x) * CORES + c
 
     barrier = pltpu.get_barrier_semaphore()
 
-    def greet(k, _):
+    def greet(peer):
         pl.semaphore_signal(
-            barrier,
-            inc=1,
-            device_id={"seq": lax.rem(me + k, seq)},
+            barrier, inc=1, device_id=peer, device_id_type=pl.DeviceIdType.MESH
+        )
+
+    def greet_seq(k, _):
+        greet({"seq": lax.rem(me + k, seq)})
+        return 0
+
+    def greet_opposite(k, _):
+        greet({"seq": k, "batch": opposite})
+        return 0
+
+    x_peers = [lax.rem(along_x + k, XS) for k in range(1, XS)]
+    z_peers = [lax.rem(along_z + k, ZS) for k in range(1, ZS)]
+    lax.fori_loop(1, seq, greet_seq, 0)
+    lax.fori_loop(0, seq, greet_opposite, 0)
+    for x in x_peers:
+        greet({"batch": batch_index(along_z, x, core)})
+    for z in z_peers:
+        greet({"batch": batch_index(z, along_x, core)})
+    greet({"batch": batch_index(along_z, along_x, 1 - core)})
+    pl.semaphore_wait(barrier, 2 * seq - 1 + XS - 1 + ZS - 1 + 1)
+
+    def side_copy(src, dst, way, peer):
+        pltpu.make_async_remote_copy(
+            src_ref=src,
+            dst_ref=dst,
+            send_sem=side_send_sem.at[way],
+            recv_sem=side_recv_sem.at[way],
+            device_id=peer,
             device_id_type=pl.DeviceIdType.MESH,
-        )
-        return 0
-
-    lax.fori_loop(1, seq, greet, 0)
-    pl.semaphore_wait(barrier, seq - 1)
+        ).start()
+
+    def wait_bytes(ref, sem):
+        pltpu.make_async_copy(ref, ref, sem).wait()
+
+    def wait_all_seq(ref, sem):
+        @pl.when(low)
+        def _():
+            wait_bytes(ref.at[pl.ds(0, seq - 1)], sem)
+
+        @pl.when(jnp.logical_not(low))
+        def _():
+            wait_bytes(ref, sem)
+
+    def scatter_filter():
+        for part in range(2):
+            for tile in range(2):
+                for line in range(8):
+                    stage[line, 8 * tile + 4 * part : 8 * tile + 4 * part + 4, :] = filter_weight[
+                        part, line, :, 128 * tile : 128 * (tile + 1)
+                    ].astype(jnp.float32)
+        tiles = []
+        for line in range(8):
+            tile = stage[jnp.where(low, line, 7 - line)]
+            tiles.append(jnp.where(low, tile, mirror_rows(tile)))
+        for to, tile in enumerate(block_transpose(tiles)):
+            scatter_send[to] = tile[:8]
+            scatter_send[8 + to] = tile[8:]
+        target = jnp.where(low, mine, opposite)
+
+        def one(k, _):
+            peer = lax.rem(me + k, seq)
+            side_copy(
+                scatter_send.at[peer], scatter_recv.at[me], 0, {"seq": peer, "batch": target}
+            )
+            return 0
+
+        @pl.when(low)
+        def _():
+            scatter_recv[me] = scatter_send[me]
+
+        lax.fori_loop(jnp.where(low, 1, 0), seq, one, 0)
+
+    def gather_z():
+        wait_all_seq(scatter_recv, side_recv_sem.at[0])
+        lane = lax.broadcasted_iota(jnp.int32, (8, 128), 1)
+        zeros = jnp.zeros((8, 128), jnp.float32)
+        moved = [pltpu.roll(scatter_recv[seq - 1 - t], 16, 1) for t in range(8)]
+        tiles = []
+        for t in range(9):
+            before = moved[t - 1] if t > 0 else zeros
+            after = moved[t] if t < 8 else zeros
+            tile = jnp.where(lane < 16, before, after)
+            tiles.append(tile + scatter_recv[t] if t < 8 else tile)
+        upper = jnp.concatenate(tiles[0:4] + [tiles[8]], axis=1)
+        lower = jnp.concatenate(tiles[4:8] + [zeros], axis=1)
+        gathered[along_z, along_x, core] = jnp.concatenate([upper, lower], axis=0).astype(
+            jnp.bfloat16
+        )
+        for z in z_peers:
+            here = gathered.at[along_z, along_x, core]
+            side_copy(here, here, 1, {"batch": batch_index(z, along_x, core)})
+
+    def gather_x():
+        wait_bytes(gathered.at[pl.ds(0, ZS - 1), 0, 0], side_recv_sem.at[1])
+        for x in x_peers:
+            here = gathered.at[:, along_x, core]
+            side_copy(here, here, 2, {"batch": batch_index(along_z, x, core)})
+
+    def gather_core():
+        wait_bytes(gathered.at[:, pl.ds(0, XS - 1), 0], side_recv_sem.at[2])
+        here = gathered.at[:, :, core]
+        side_copy(here, here, 3, {"batch": batch_index(along_z, along_x, 1 - core)})
+
+    def gather_finish():
+        wait_bytes(gathered.at[:, :, 0], side_recv_sem.at[3])
+        whole = gathered[...].reshape(batch * 16, 640)
+        for h in range(2):
+            piece = dot(spread[h], whole[:, :512]).astype(jnp.bfloat16).T.astype(jnp.float32)
+            field[512 * h : 512 * (h + 1), :] = piece[:, :F2]
+            field[1024 + 512 * h : 1024 + 512 * (h + 1), :] = piece[:, F2:]
+        piece = dot(spread[0], whole[:, 512:]).astype(jnp.bfloat16).T
+        filt_mid[...] = piece[:feats]
+        for d in range(feats):
+            real = field[pl.ds(d, LINES, stride=feats), :]
+            imag = field[pl.ds(1024 + d, LINES, stride=feats), :]
+            filt[d * LINES : (d + 1) * LINES, :] = jnp.concatenate([real, imag], axis=1).astype(
+                jnp.bfloat16
+            )
+
+    def reduce_core():
+        parts = []
+        for h in range(2):
+            real = grad_field[512 * h : 512 * (h + 1), :]
+            imag = grad_field[1024 + 512 * h : 1024 + 512 * (h + 1), :]
+            both = jnp.concatenate([real, imag], axis=1).astype(jnp.bfloat16)
+            parts.append(dot_nt(collect[...], both).reshape(batch, 8, 512))
+        mid = jnp.concatenate(
+            [grad_mid[...], jnp.zeros((128 - feats, 2 * F2), jnp.float32)], axis=0
+        ).astype(jnp.bfloat16)
+        last = dot_nt(collect[...], mid).reshape(batch, 8, 128)
+        both = jnp.concatenate(
+            [
+                jnp.concatenate(parts, axis=1),
+                jnp.concatenate([last, jnp.zeros_like(last)], axis=1),
+            ],
+            axis=2,
+        )
+        core_send[...] = both.astype(jnp.bfloat16).reshape(ZS, XS, CORES, 16, 640)
+        side_copy(
+            core_send.at[:, :, 1 - core],
+            core_recv,
+            4,
+            {"batch": batch_index(along_z, along_x, 1 - core)},
+        )
+
+    def reduce_x():
+        wait_bytes(core_recv, side_recv_sem.at[4])
+        own = core_send[:, :, core].astype(jnp.float32) + core_recv[...].astype(jnp.float32)
+        x_send[...] = own.astype(jnp.bfloat16)
+        x_recv[along_x] = x_send[:, along_x]
+        for x in x_peers:
+            side_copy(
+                x_send.at[:, x], x_recv.at[along_x], 5, {"batch": batch_index(along_z, x, core)}
+            )
+
+    def reduce_z():
+        wait_bytes(x_recv.at[pl.ds(0, XS - 1)], side_recv_sem.at[5])
+        z_send[...] = jnp.sum(x_recv[...].astype(jnp.float32), axis=0).astype(jnp.bfloat16)
+        z_recv[along_z] = z_send[along_z]
+        for z in z_peers:
+            side_copy(
+                z_send.at[z], z_recv.at[along_z], 6, {"batch": batch_index(z, along_x, core)}
+            )
+
+    def return_grad():
+        wait_bytes(z_recv.at[pl.ds(0, ZS - 1)], side_recv_sem.at[6])
+        total = jnp.sum(z_recv[...].astype(jnp.float32), axis=0)
+        tiles = [total[:8, 128 * t : 128 * (t + 1)] for t in range(4)]
+        tiles += [total[8:, 128 * t : 128 * (t + 1)] for t in range(4)]
+        tiles.append(total[:8, 512:])
+        lane = lax.broadcasted_iota(jnp.int32, (8, 128), 1)
+        moved = [pltpu.roll(t, 112, 1) for t in tiles]
+        for t in range(8):
+            return_send[t] = tiles[t]
+            return_send[seq - 1 - t] = jnp.where(lane < 112, moved[t], moved[t + 1])
+
+        def one(k, _):
+            peer = lax.rem(me + k, seq)
+            target = jnp.where(peer < seq // 2, mine, opposite)
+            side_copy(
+                return_send.at[peer], return_recv.at[me], 7, {"seq": peer, "batch": target}
+            )
+            return 0
+
+        @pl.when(low)
+        def _():
+            return_recv[me] = return_send[me]
+
+        lax.fori_loop(jnp.where(low, 1, 0), seq, one, 0)
+
+    def return_finish():
+        wait_all_seq(return_recv, side_recv_sem.at[7])
+        tiles = [
+            jnp.concatenate([return_recv[t], return_recv[8 + t]], axis=0) for t in range(8)
+        ]
+        for line, tile in enumerate(block_transpose(tiles)):
+            stage[jnp.where(low, line, 7 - line)] = jnp.where(low, tile, mirror_rows(tile))
+        for part in range(2):
+            for tile in range(2):
+                for line in range(8):
+                    filter_grad[part, line, :, 128 * tile : 128 * (tile + 1)] = stage[
+                        line, 8 * tile + 4 * part : 8 * tile + 4 * part + 4, :
+                    ]
+
+    def side_drain():
+        wait_all_seq(scatter_send, side_send_sem.at[0])
+        wait_bytes(gathered.at[pl.ds(0, ZS - 1), 0, 0], side_send_sem.at[1])
+        wait_bytes(gathered.at[:, pl.ds(0, XS - 1), 0], side_send_sem.at[2])
+        wait_bytes(gathered.at[:, :, 0], side_send_sem.at[3])
+        wait_bytes(core_recv, side_send_sem.at[4])
+        wait_bytes(x_recv.at[pl.ds(0, XS - 1)], side_send_sem.at[5])
+        wait_bytes(z_recv.at[pl.ds(0, ZS - 1)], side_send_sem.at[6])
+        wait_all_seq(return_send, side_send_sem.at[7])
 
     def exchange(src, dst, way, chunk):
         def one(k, _):
@@ -184,7 +452,7 @@
                     )
             spectrum = dot(jnp.concatenate(halves, axis=0), inner_fwd[...])
             where = pl.ds(pl.multiple_of(base * LINES, 4 * LINES), 4 * LINES)
-            product = multiply(spectrum, where)
+            product = multiply(spectrum, where, base)
             half = dot(product, inner_inv[...])
             for sub in range(2):
                 columns = []
@@ -229,7 +497,7 @@
         fr, fi = split(f)
         return jnp.concatenate([fr * zr + fi * zi, fr * zi - fi * zr], axis=1)
 
-    def filter_main(z, where):
+    def filter_main(z, where, feature):
         z = z.astype(jnp.bfloat16)
         spec[where, :] = z
         return times(z, filt[where, :])
@@ -239,18 +507,27 @@
         spec_mid[...] = z
         return times(z, filt_mid[...])
 
-    def back_main(z, where):
+    def back_main(z, where, feature):
         z = z.astype(jnp.bfloat16)
-        grad[where, :] = (times_conj(z, spec[where, :]) * inv_length).astype(jnp.bfloat16)
+        term = times_conj(z, spec[where, :]) * inv_length
+        for i in range(4):
+            piece = term[i * LINES : (i + 1) * LINES]
+            grad_field[pl.ds(feature + i, LINES, stride=feats), :] = piece[:, :F2]
+            grad_field[pl.ds(1024 + feature + i, LINES, stride=feats), :] = piece[:, F2:]
         return times_conj(z, filt[where, :]).astype(jnp.bfloat16)
 
     def back_mid(z):
         z = z.astype(jnp.bfloat16)
-        grad_mid[...] = (times_conj(z, spec_mid[...]) * inv_length).astype(jnp.bfloat16)
+        grad_mid[...] = times_conj(z, spec_mid[...]) * inv_length
         return times_conj(z, filt_mid[...]).astype(jnp.bfloat16)
 
+    scatter_filter()
     for chunk in range(chunks):
         send_positions(lambda j: history[pl.ds(j * F2, F2), :], 0, chunk)
+    gather_z()
+    gather_x()
+    gather_core()
+    gather_finish()
     for chunk in range(chunks):
         wait_chunk(0, chunk)
     transform(0, filter_main, filter_mid)
@@ -281,6 +558,10 @@
     transform(1, back_main, back_mid)
     for chunk in range(chunks):
         send_features(1, chunk)
+    reduce_core()
+    reduce_x()
+    reduce_z()
+    return_grad()
     for chunk in range(chunks):
         wait_chunk(3, chunk)
         for j in range(chunk * CHUNK, (chunk + 1) * CHUNK):
@@ -288,6 +569,8 @@
             part = pl.ds(j * F2, F2)
             out[part, :] = (grad_rows[part, :] + back).astype(jnp.bfloat16)
 
+    return_finish()
+    side_drain()
     sent = send_in.at[0, :, pl.ds(0, seq - 1)]
     for way in range(4):
         pltpu.make_async_copy(sent, sent, send_sem.at[way]).wait()
@@ -301,27 +584,17 @@
     bf16, f32 = jnp.bfloat16, jnp.float32
     tables = [jnp.asarray(t) for t in host_tables()]
 
-    full = lax.all_to_all(filter_weight, "seq", split_axis=3, concat_axis=1, tiled=True)
-    full = lax.all_gather(full, "batch", axis=2, tiled=True)
-    mirrored = jnp.flip(full[:, LINES:], axis=(1, 2)).astype(f32) * jnp.array(
-        [1.0, -1.0], f32
-    ).reshape(2, 1, 1, 1)
-    main = full[:, :LINES].astype(f32) + jnp.pad(
-        mirrored[:, : LINES - 1], ((0, 0), (1, 0), (0, 0), (0, 0))
-    )
-    filt = main.astype(bf16).transpose(3, 1, 0, 2).reshape(feats * LINES, 2 * F2)
-    filt_mid = mirrored[:, LINES - 1].astype(bf16).transpose(2, 0, 1).reshape(feats, 2 * F2)
-
     vmem = pl.BlockSpec(memory_space=pltpu.VMEM)
-    out, grad, grad_mid = pl.pallas_call(
-        functools.partial(kernel, seq),
+    batch = lax.axis_size("batch")
+    dma = pltpu.SemaphoreType.DMA
+    out, filter_grad = pl.pallas_call(
+        functools.partial(kernel, seq, batch),
         out_shape=(
             jax.ShapeDtypeStruct((row_count, features), bf16),
-            jax.ShapeDtypeStruct((feats * LINES, 2 * F2), bf16),
-            jax.ShapeDtypeStruct((feats, 2 * F2), bf16),
+            jax.ShapeDtypeStruct(filter_weight.shape, f32),
         ),
-        in_specs=[vmem] * 15,
-        out_specs=(vmem,) * 3,
+        in_specs=[vmem] * 16,
+        out_specs=(vmem,) * 2,
         scratch_shapes=[
             pltpu.VMEM((2, rows, seq, feats, F2), bf16),
             pltpu.VMEM((2, seq, rows, feats, F2), bf16),
@@ -329,10 +602,28 @@
             pltpu.VMEM((2, rows, seq, feats, F2), bf16),
             pltpu.VMEM((feats * LINES, 2 * F2), bf16),
             pltpu.VMEM((feats, 2 * F2), bf16),
+            pltpu.VMEM((feats * LINES, 2 * F2), bf16),
+            pltpu.VMEM((feats, 2 * F2), bf16),
             pltpu.VMEM((F1 * feats, F2), f32),
+            pltpu.VMEM((2 * LINES * feats, F2), f32),
+            pltpu.VMEM((feats, 2 * F2), f32),
             pltpu.VMEM((row_count, features), f32),
-            pltpu.SemaphoreType.DMA((4,)),
-            pltpu.SemaphoreType.DMA((4, rows // CHUNK)),
+            pltpu.VMEM((8, 16, 128), f32),
+            pltpu.VMEM((seq, 8, 128), f32),
+            pltpu.VMEM((seq, 8, 128), f32),
+            pltpu.VMEM((ZS, XS, CORES, 16, 640), bf16),
+            pltpu.VMEM((ZS, XS, CORES, 16, 640), bf16),
+            pltpu.VMEM((ZS, XS, 16, 640), bf16),
+            pltpu.VMEM((ZS, XS, 16, 640), bf16),
+            pltpu.VMEM((XS, ZS, 16, 640), bf16),
+            pltpu.VMEM((ZS, 16, 640), bf16),
+            pltpu.VMEM((ZS, 16, 640), bf16),
+            pltpu.VMEM((seq, 8, 128), f32),
+            pltpu.VMEM((seq, 8, 128), f32),
+            dma((4,)),
+            dma((4, rows // CHUNK)),
+            dma((8,)),
+            dma((8,)),
         ],
         compiler_params=pltpu.CompilerParams(
             collective_id=0, has_side_effects=True, vmem_limit_bytes=48 * 2**20
@@ -340,8 +631,7 @@
     )(
         history.reshape(row_count, features),
         cotangent.reshape(row_count, features),
-        filt,
-        filt_mid,
+        filter_weight,
         gain_first.reshape(1, features),
         bias_first.reshape(1, features),
         w_in,
@@ -349,18 +639,7 @@
         gain_second.reshape(1, features),
         *tables
     )
-    half = jnp.concatenate(
-        [
-            grad.reshape(feats, LINES, 2, F2).transpose(2, 1, 3, 0),
-            grad_mid.reshape(feats, 1, 2, F2).transpose(2, 1, 3, 0),
-        ],
-        axis=1,
-    )
-    sign = jnp.array([1.0, -1.0], bf16).reshape(2, 1, 1, 1)
-    whole = jnp.concatenate([half, jnp.flip(half[:, 1:LINES], axis=(1, 2)) * sign], axis=1)
-    part = lax.psum_scatter(whole, "batch", scatter_dimension=2, tiled=True)
-    filter_grad = lax.all_to_all(part, "seq", split_axis=1, concat_axis=3, tiled=True)
-    return (out.reshape(user_count, row_count, features), filter_grad.astype(f32))
+    return (out.reshape(user_count, row_count, features), filter_grad)
 
 
 def solution(mesh):

time: 311 us -> 118 us (0.38); the launches traced: 305 us -> 117 us
  waiting for transfers between devices: 188 us -> 0 us
  Pallas kernels: 59.2 us -> 103 us
  between operations: 14.4 us -> 0.69 us
  blocking collectives: 13.2 us -> 0 us
  local copies, waits for them, and re-layouts: 23.2 us -> 13 us
  starting transfers between devices: 4.64 us -> 0 us
    reduce_scatter x1 -> x0, waiting for transfers between devices: 108 us -> none  [local(): part = lax.psum_scatter(whole, 'batch', scatter_dimension=2, tiled=True)]
    all_gather x1 -> x0, waiting for transfers between devices: 75 us -> none  [local(): full = lax.all_gather(full, 'batch', axis=2, tiled=True)]
    pallas_call x1, Pallas kernels: 59.2 us -> 103 us  [local(): pl.pallas_call(functools.partial(kernel, seq, batch), out_shape=(jax.Shap...]
    all_to_all x1 -> x0, blocking collectives: 13.2 us -> none  [local(): lax.all_to_all(filter_weight, 'seq', split_axis=3, concat_axis=1, tiled=T...]
    all_to_all x1 -> x0, waiting for transfers between devices: 5.16 us -> none  [local(): lax.all_to_all(part, 'seq', split_axis=1, concat_axis=3, tiled=True)]
    all_to_all x1 -> x0, starting transfers between devices: 4.56 us -> none  [local(): lax.all_to_all(part, 'seq', split_axis=1, concat_axis=3, tiled=True)]
    unnamed x41 -> x34, local copies, waits for them, and re-layouts: 8.92 us -> 13 us
    reshape x5 -> x0, local copies, waits for them, and re-layouts: 3.82 us -> none  [the longest x2 2.59 us: local(): grad_mid.reshape(feats, 1, 2, F2).transpose(2, 1, 3, 0)]
  transfers between devices with their start and end apart: 3 -> 0, of which waited for: 3 -> 0; matrix products, arithmetic and copies ran while one was open for 0% -> 0% of each run, Pallas kernels for 0% -> 0%
where the time goes in v2:
time: 118 us; the launch traced here: 117 us
  Pallas kernels  103 us (87%)
  local copies, waits for them, and re-layouts  13 us (11%)
    pallas_call x1, Pallas kernels, local(): pl.pallas_call(functools.partial(kernel, seq, batch), out_shape=(jax.Shap...  103 us
    unnamed x34, local copies, waits for them, and re-layouts  13 us

profile of v2, /device:TPU:25, one launch (start us, length us, event | category | flops | bytes accessed | tf_op | source)
XLA Modules:
  0.0 117.0 jit_solution(15057512933767101075)
XLA Ops:
  0.6 0.0 copy-start.15
  0.6 0.0 copy-start.13
  0.7 0.0 copy-start.14
  0.7 0.0 copy-start.12
  0.7 0.6 copy-done.15
  1.3 0.0 copy-done.13
  1.3 0.0 copy-done.14
  1.3 0.0 copy-done.12
  1.4 0.0 copy-start
  1.4 1.0 copy-done
  2.4 0.0 copy-start.1
  2.4 1.0 copy-done.1
  3.4 0.0 copy-start.2
  3.4 1.0 copy-done.2
  4.5 0.0 copy-start.3
  4.5 0.9 copy-done.3
  5.4 0.0 copy-start.4
  5.4 0.9 copy-done.4
  6.4 0.0 copy-start.5
  6.4 0.9 copy-done.5
  7.3 0.0 copy-start.6
  7.3 0.9 copy-done.6
  8.2 0.0 copy-start.7
  8.2 0.9 copy-done.7
  9.1 0.0 copy-start.8
  9.1 0.8 copy-done.8
  9.9 0.0 copy-start.9
  9.9 0.8 copy-done.9
  10.7 0.0 copy-start.10
  10.7 0.8 copy-done.10
  11.5 0.0 copy-start.11
  11.5 0.8 copy-done.11
  12.2 103.3 %shard_map.167 = (bf16[1024,256]{1,0:T(8,128)(2,1)S(1)}, f32[2,8,4,256]{3,2,1,0:T(4,128)S(1)}) custom-call(bf16[1024,256]{1,0:T(8,128)(2,1)S(1)} %bitcast.7, bf16[1024,256]{1,0:T(8,128)(2,1)S(1)} %bitcast.8, bf16[2,8,4,256]{3,2,1,0:T(4,128)(2,1)S(1)} %copy-done.9, f32[1,256]{1,0:T(1,128)S(1)} %bitcast.9, f32[1,256]{1,0:T(1,128)S(1)} %bitcast.10, ...), custom_call_target="tpu_custom_call" | custom-call | tf_op jit(solution)/shard_map/pallas_call | solution.py:590
  115.5 0.8 copy.20
  116.3 0.6 copy.21
Async XLA Ops:
  0.6 0.7 copy-start.15
  0.6 0.7 copy-start.13
  0.7 0.7 copy-start.14
  0.7 0.7 copy-start.12
  1.4 1.0 copy-start
  2.4 1.0 copy-start.1
  3.4 1.0 copy-start.2
  4.5 0.9 copy-start.3
  5.4 0.9 copy-start.4
  6.4 0.9 copy-start.5
  7.3 0.9 copy-start.6
  8.2 0.9 copy-start.7
  9.1 0.8 copy-start.8
  9.9 0.8 copy-start.9
  10.7 0.8 copy-start.10
  11.5 0.8 copy-start.11

commit v3 on v2

v3 whole, which is shorter than its diff:
```python
import functools
import math

import jax
import jax.numpy as jnp
import ml_dtypes
import numpy as np
from jax import lax
from jax.experimental import pallas as pl
from jax.experimental.pallas import tpu as pltpu
from jax.sharding import PartitionSpec as P

F1 = 128
F2 = 128
LINES = 64
CHUNK = 2
ZS, XS, CORES = 4, 4, 2

epsilon = 1e-05
inv_root_two = 1.0 / math.sqrt(2.0)
inv_root_tau = 1.0 / math.sqrt(2.0 * math.pi)
inv_length = 1.0 / (F1 * F2)


def columns(table):
    blocks = np.split(table, table.shape[1] // 128, axis=1)
    return np.stack(blocks).astype(ml_dtypes.bfloat16)


def whole(table):
    return jnp.concatenate([table[k] for k in range(table.shape[0])], axis=1)


def host_tables():
    index = np.arange(F1)
    angle = 2.0 * np.pi * (index[:, None] * index[None, :] % F1) / F1
    cos, sin = np.cos(angle), np.sin(angle)
    outer_fwd = np.concatenate([cos[:LINES], -sin[:LINES]], axis=0)
    outer_inv = np.concatenate([cos[:LINES], -sin[:LINES]], axis=0).T
    inner_fwd = np.block([[cos, -sin], [sin, cos]])
    inner_inv = np.block([[cos, sin], [-sin, cos]])
    lines = np.arange(LINES + 1)
    phase = 2.0 * np.pi * (lines[:, None] * index[None, :]) / (F1 * F2)
    narrow = [columns(t) for t in (outer_fwd, outer_inv, inner_fwd, inner_inv)]
    twiddles = np.stack([np.cos(phase), np.sin(phase)]).astype(np.float32)
    return (*narrow, twiddles[:, :LINES], twiddles[:, LINES:], *permutations())


def permutations():
    spread = np.zeros((2, 2 * F2, 4 * F2), np.float32)
    collect = np.zeros((2 * F2, 2 * F2), np.float32)
    for part in range(2):
        for q in range(F2):
            for h in range(2):
                spread[h, part * F2 + q, (q // 4) * 16 + h * 8 + part * 4 + q % 4] = 1.0
            collect[(q // 4) * 8 + part * 4 + q % 4, part * F2 + q] = 1.0
    return columns(spread.reshape(4 * F2, 4 * F2)), columns(collect)


def dot(a, b):
    return jnp.dot(a, b, preferred_element_type=jnp.float32)


def dot_nt(a, b):
    return lax.dot_general(a, b, (((1,), (1,)), ((), ())), preferred_element_type=jnp.float32)


def mirror_rows(x):
    axis = x.ndim - 2
    size = x.shape[axis]
    row = lax.broadcasted_iota(jnp.int32, x.shape, axis)
    for step in (1, 2):
        up, down = pltpu.roll(x, step, axis), pltpu.roll(x, size - step, axis)
        x = jnp.where((row & step) != 0, up, down)
    return jnp.where((row & 4) != 0, -x, x)


def block_transpose(tiles):
    lane = lax.broadcasted_iota(jnp.int32, tiles[0].shape, 1) // 16
    result = []
    for to in range(8):
        total = tiles[to]
        for block in range(8):
            if block != to:
                moved = pltpu.roll(tiles[block], 16 * ((block - to) % 8), 1)
                total = jnp.where(lane == block, moved, total)
        result.append(total)
    return result


def mean(x):
    return jnp.mean(x, axis=-1, keepdims=True)


def local_rows(mixed, history, cot, gain_first, bias_first, w_in, w_out, gain_second):
    summed = mixed + history.astype(jnp.float32)
    center_one = summed - mean(summed)
    inv_one = lax.rsqrt(mean(center_one * center_one) + epsilon)
    norm_one = center_one * inv_one
    hidden = (norm_one * gain_first + bias_first).astype(jnp.bfloat16)
    preact = dot(hidden, w_in)
    cumul = 0.5 * (1.0 + lax.erf(preact * inv_root_two))
    activation = (preact * cumul).astype(jnp.bfloat16)
    output_sum = dot(activation, w_out) + hidden.astype(jnp.float32)
    center_two = output_sum - mean(output_sum)
    inv_two = lax.rsqrt(mean(center_two * center_two) + epsilon)
    norm_two = center_two * inv_two
    grad_norm = cot.astype(jnp.float32) * gain_second
    grad_sum = inv_two * (grad_norm - mean(grad_norm) - norm_two * mean(grad_norm * norm_two))
    grad_act = dot_nt(grad_sum.astype(jnp.bfloat16), w_out)
    density = jnp.exp(-0.5 * preact * preact) * inv_root_tau
    grad_pre = (grad_act * (cumul + preact * density)).astype(jnp.bfloat16)
    grad_hidden = dot_nt(grad_pre, w_in) + grad_sum
    grad_scaled = grad_hidden * gain_first
    return inv_one * (grad_scaled - mean(grad_scaled) - norm_one * mean(grad_scaled * norm_one))


def kernel(
    seq,
    batch,
    history_hbm,
    cotangent_hbm,
    filter_weight_hbm,
    gain_first_hbm,
    bias_first_hbm,
    w_in_hbm,
    w_out_hbm,
    gain_second_hbm,
    outer_fwd_hbm,
    outer_inv_hbm,
    inner_fwd_hbm,
    inner_inv_hbm,
    twiddle_hbm,
    twiddle_mid_hbm,
    spread_hbm,
    collect_hbm,
    out_hbm,
    filter_grad_hbm,
    history,
    cotangent,
    filter_weight,
    gain_first,
    bias_first,
    w_in,
    w_out,
    gain_second,
    outer_fwd,
    outer_inv,
    inner_fwd,
    inner_inv,
    twiddle,
    twiddle_mid,
    spread,
    collect,
    out,
    filter_grad,
    send_in,
    send_out,
    recv_in,
    recv_out,
    spec,
    spec_mid,
    back_spec,
    back_mid,
    filt,
    filt_mid,
    field,
    grad_field,
    grad_rows,
    stage,
    scatter_send,
    scatter_recv,
    gathered,
    core_send,
    core_recv,
    x_send,
    x_half,
    x_recv,
    z_send,
    z_half_left,
    z_half_right,
    z_recv,
    return_send,
    return_recv,
    load_sem,
    store_sem,
    send_sem,
    recv_sem,
    side_send_sem,
    side_recv_sem,
):
    me = lax.axis_index("seq")
    mine = lax.axis_index("batch")
    rows = F1 // seq
    feats = history.shape[1] // seq
    chunks = rows // CHUNK
    core = lax.rem(mine, CORES)
    along_x = lax.rem(mine // CORES, XS)
    along_z = mine // (CORES * XS)
    opposite = batch - 1 - mine
    low = me < seq // 2

    def batch_index(z, x, c):
        return (z * XS + x) * CORES + c

    x_right, x_left, x_far = (lax.rem(along_x + k, XS) for k in (1, XS - 1, 2))
    z_right, z_left, z_far = (lax.rem(along_z + k, ZS) for k in (1, ZS - 1, 2))
    to_x_right = {"batch": batch_index(along_z, x_right, core)}
    to_x_left = {"batch": batch_index(along_z, x_left, core)}
    to_z_right = {"batch": batch_index(z_right, along_x, core)}
    to_z_left = {"batch": batch_index(z_left, along_x, core)}
    to_core = {"batch": batch_index(along_z, along_x, 1 - core)}

    loads = {}
    for name, source, target in (
        ("filter", filter_weight_hbm, filter_weight),
        ("history", history_hbm, history),
        ("outer_fwd", outer_fwd_hbm, outer_fwd),
        ("twiddle", twiddle_hbm, twiddle),
        ("twiddle_mid", twiddle_mid_hbm, twiddle_mid),
        ("inner_fwd", inner_fwd_hbm, inner_fwd),
        ("spread", spread_hbm, spread),
        ("inner_inv", inner_inv_hbm, inner_inv),
        ("outer_inv", outer_inv_hbm, outer_inv),
        ("gain_first", gain_first_hbm, gain_first),
        ("bias_first", bias_first_hbm, bias_first),
        ("w_in", w_in_hbm, w_in),
        ("w_out", w_out_hbm, w_out),
        ("gain_second", gain_second_hbm, gain_second),
        ("cotangent", cotangent_hbm, cotangent),
        ("collect", collect_hbm, collect),
    ):
        loads[name] = pltpu.make_async_copy(source, target, load_sem.at[len(loads)])
        loads[name].start()

    barrier = pltpu.get_barrier_semaphore()

    def greet(peer):
        pl.semaphore_signal(
            barrier, inc=1, device_id=peer, device_id_type=pl.DeviceIdType.MESH
        )

    def greet_seq(k, _):
        greet({"seq": lax.rem(me + k, seq)})
        return 0

    def greet_opposite(k, _):
        greet({"seq": k, "batch": opposite})
        return 0

    lax.fori_loop(0, seq, greet_opposite, 0)
    for peer in (to_x_right, to_x_left, to_z_right, to_z_left, to_core):
        greet(peer)
    lax.fori_loop(1, seq, greet_seq, 0)

    def side_copy(src, dst, way, peer):
        pltpu.make_async_remote_copy(
            src_ref=src,
            dst_ref=dst,
            send_sem=side_send_sem.at[way],
            recv_sem=side_recv_sem.at[way],
            device_id=peer,
            device_id_type=pl.DeviceIdType.MESH,
        ).start()

    def wait_bytes(ref, sem):
        pltpu.make_async_copy(ref, ref, sem).wait()

    def wait_all_seq(ref, sem):
        @pl.when(low)
        def _():
            wait_bytes(ref.at[pl.ds(0, seq - 1)], sem)

        @pl.when(jnp.logical_not(low))
        def _():
            wait_bytes(ref, sem)

    piece = gathered.at[0, 0, 0]
    sizes = {
        1: piece,
        2: piece,
        3: piece.at[pl.ds(0, 3)],
        4: piece.at[pl.ds(0, 2)],
        5: gathered.at[:, 0, 0],
        6: gathered.at[:, 0, 0],
        7: gathered.at[pl.ds(0, 2), 0, 0],
        8: gathered.at[pl.ds(0, 2), 0, 0],
        9: gathered.at[:, :, 0],
        10: core_recv,
        11: x_half.at[0],
        12: x_half.at[0],
        13: x_recv.at[0],
        14: x_recv.at[0],
        15: z_half_left,
        16: z_half_right,
        17: z_recv.at[0],
        18: z_recv.at[0],
    }

    def arrived(*ways):
        for way in ways:
            wait_bytes(sizes[way], side_recv_sem.at[way])

    def scatter_prepare():
        for part in range(2):
            for tile in range(2):
                for line in range(8):
                    stage[line, 8 * tile + 4 * part : 8 * tile + 4 * part + 4, :] = filter_weight[
                        part, line, :, 128 * tile : 128 * (tile + 1)
                    ].astype(jnp.float32)
        tiles = []
        for line in range(8):
            tile = stage[jnp.where(low, line, 7 - line)]
            tiles.append(jnp.where(low, tile, mirror_rows(tile)))
        for to, tile in enumerate(block_transpose(tiles)):
            scatter_send[to] = tile[:8]
            scatter_send[8 + to] = tile[8:]

    def scatter_start():
        target = jnp.where(low, mine, opposite)

        def one(k, _):
            peer = lax.rem(me + k, seq)
            side_copy(
                scatter_send.at[peer], scatter_recv.at[me], 0, {"seq": peer, "batch": target}
            )
            return 0

        @pl.when(low)
        def _():
            scatter_recv[me] = scatter_send[me]

        lax.fori_loop(jnp.where(low, 1, 0), seq, one, 0)

    def gather():
        wait_all_seq(scatter_recv, side_recv_sem.at[0])
        lane = lax.broadcasted_iota(jnp.int32, (8, 128), 1)
        zeros = jnp.zeros((8, 128), jnp.float32)
        moved = [pltpu.roll(scatter_recv[seq - 1 - t], 16, 1) for t in range(8)]
        tiles = []
        for t in range(9):
            before = moved[t - 1] if t > 0 else zeros
            after = moved[t] if t < 8 else zeros
            tile = jnp.where(lane < 16, before, after)
            tiles.append(tile + scatter_recv[t] if t < 8 else tile)
        for t in range(5):
            upper = tiles[t] if t < 4 else tiles[8]
            lower = tiles[4 + t] if t < 4 else zeros
            gathered[along_z, along_x, core, t] = jnp.concatenate([upper, lower], axis=0).astype(
                jnp.bfloat16
            )
        own = gathered.at[along_z, along_x, core]
        side_copy(own, own, 1, to_z_right)
        side_copy(own, own, 2, to_z_left)
        arrived(1)
        block = gathered.at[z_left, along_x, core, pl.ds(0, 3)]
        side_copy(block, block, 3, to_z_right)
        arrived(2)
        block = gathered.at[z_right, along_x, core, pl.ds(3, 2)]
        side_copy(block, block, 4, to_z_left)
        arrived(3, 4)
        block = gathered.at[:, along_x, core]
        side_copy(block, block, 5, to_x_right)
        side_copy(block, block, 6, to_x_left)
        arrived(5)
        block = gathered.at[pl.ds(0, 2), x_left, core]
        side_copy(block, block, 7, to_x_right)
        arrived(6)
        block = gathered.at[pl.ds(2, 2), x_right, core]
        side_copy(block, block, 8, to_x_left)
        arrived(7, 8)
        block = gathered.at[:, :, core]
        side_copy(block, block, 9, to_core)
        arrived(9)
        loads["spread"].wait()
        parts = [gathered[:, :, :, t].reshape(batch * 16, 128) for t in range(5)]
        block = jnp.concatenate(parts[:4], axis=1)
        for h in range(2):
            table = jnp.concatenate(
                [spread[k, 2 * F2 * h : 2 * F2 * (h + 1)] for k in range(4)], axis=1
            )
            result = dot(table, block).astype(jnp.bfloat16).T.astype(jnp.float32)
            field[512 * h : 512 * (h + 1), :] = result[:, :F2]
            field[1024 + 512 * h : 1024 + 512 * (h + 1), :] = result[:, F2:]
        table = jnp.concatenate([spread[k, : 2 * F2] for k in range(4)], axis=1)
        filt_mid[...] = dot(table, parts[4]).astype(jnp.bfloat16).T[:feats]
        for d in range(feats):
            real = field[pl.ds(d, LINES, stride=feats), :]
            imag = field[pl.ds(1024 + d, LINES, stride=feats), :]
            filt[d * LINES : (d + 1) * LINES, :] = jnp.concatenate([real, imag], axis=1).astype(
                jnp.bfloat16
            )

    def reduce_start():
        for d in range(feats):
            where = pl.ds(d * LINES, LINES)
            term = times_conj(back_spec[where, :], spec[where, :]) * inv_length
            grad_field[pl.ds(d, LINES, stride=feats), :] = term[:, :F2]
            grad_field[pl.ds(1024 + d, LINES, stride=feats), :] = term[:, F2:]
        loads["collect"].wait()
        parts = []
        for h in range(2):
            real = grad_field[512 * h : 512 * (h + 1), :]
            imag = grad_field[1024 + 512 * h : 1024 + 512 * (h + 1), :]
            both = jnp.concatenate([real, imag], axis=1).astype(jnp.bfloat16)
            parts.append(dot_nt(whole(collect), both).reshape(batch, 8, 512))
        mid = jnp.concatenate(
            [
                times_conj(back_mid[...], spec_mid[...]) * inv_length,
                jnp.zeros((128 - feats, 2 * F2), jnp.float32),
            ],
            axis=0,
        ).astype(jnp.bfloat16)
        last = dot_nt(whole(collect), mid).reshape(batch, 8, 128)
        both = jnp.concatenate(parts, axis=1).astype(jnp.bfloat16)
        both = both.reshape(ZS, XS, CORES, 16, 512)
        for t in range(4):
            core_send[:, :, :, t] = both[..., 128 * t : 128 * (t + 1)]
        last = jnp.concatenate([last, jnp.zeros_like(last)], axis=1).astype(jnp.bfloat16)
        core_send[:, :, :, 4] = last.reshape(ZS, XS, CORES, 16, 128)
        side_copy(core_send.at[:, :, 1 - core], core_recv, 10, to_core)

    def add(a, b):
        return (a.astype(jnp.float32) + b.astype(jnp.float32)).astype(jnp.bfloat16)

    def reduce_x():
        arrived(10)
        for x in range(XS):
            x_send[x] = add(core_send[:, x, core], core_recv[:, x])
        side_copy(x_send.at[x_far, pl.ds(0, 2)], x_half.at[0], 11, to_x_right)
        side_copy(x_send.at[x_far, pl.ds(2, 2)], x_half.at[1], 12, to_x_left)

    def reduce_x_second():
        arrived(11)
        x_send[x_right, 0:2] = add(x_send[x_right, 0:2], x_half[0])
        side_copy(x_send.at[x_right], x_recv.at[0], 13, to_x_right)
        arrived(12)
        x_send[x_left, 2:4] = add(x_send[x_left, 2:4], x_half[1])
        side_copy(x_send.at[x_left], x_recv.at[1], 14, to_x_left)

    def reduce_z():
        arrived(13, 14)
        total = x_send[along_x].astype(jnp.float32) + x_recv[0].astype(jnp.float32)
        z_send[...] = (total + x_recv[1].astype(jnp.float32)).astype(jnp.bfloat16)
        side_copy(z_send.at[z_far, pl.ds(0, 3)], z_half_left, 15, to_z_right)
        side_copy(z_send.at[z_far, pl.ds(3, 2)], z_half_right, 16, to_z_left)

    def reduce_z_second():
        arrived(15)
        z_send[z_right, 0:3] = add(z_send[z_right, 0:3], z_half_left[...])
        side_copy(z_send.at[z_right], z_recv.at[0], 17, to_z_right)
        arrived(16)
        z_send[z_left, 3:5] = add(z_send[z_left, 3:5], z_half_right[...])
        side_copy(z_send.at[z_left], z_recv.at[1], 18, to_z_left)

    def return_grad():
        arrived(17, 18)
        total = z_send[along_z].astype(jnp.float32) + z_recv[0].astype(jnp.float32)
        total = total + z_recv[1].astype(jnp.float32)
        tiles = [total[t, :8] for t in range(4)] + [total[t, 8:] for t in range(4)]
        tiles.append(total[4, :8])
        lane = lax.broadcasted_iota(jnp.int32, (8, 128), 1)
        moved = [pltpu.roll(t, 112, 1) for t in tiles]
        for t in range(8):
            return_send[t] = tiles[t]
            return_send[seq - 1 - t] = jnp.where(lane < 112, moved[t], moved[t + 1])

        def one(k, _):
            peer = lax.rem(me + k, seq)
            target = jnp.where(peer < seq // 2, mine, opposite)
            side_copy(
                return_send.at[peer], return_recv.at[me], 19, {"seq": peer, "batch": target}
            )
            return 0

        @pl.when(low)
        def _():
            return_recv[me] = return_send[me]

        lax.fori_loop(jnp.where(low, 1, 0), seq, one, 0)

    def return_finish():
        wait_all_seq(return_recv, side_recv_sem.at[19])
        tiles = [
            jnp.concatenate([return_recv[t], return_recv[8 + t]], axis=0) for t in range(8)
        ]
        for line, tile in enumerate(block_transpose(tiles)):
            stage[jnp.where(low, line, 7 - line)] = jnp.where(low, tile, mirror_rows(tile))
        for part in range(2):
            for tile in range(2):
                for line in range(8):
                    filter_grad[part, line, :, 128 * tile : 128 * (tile + 1)] = stage[
                        line, 8 * tile + 4 * part : 8 * tile + 4 * part + 4, :
                    ]

    def exchange(src, dst, way, chunk):
        def one(k, _):
            peer = lax.rem(me + k, seq)
            pltpu.make_async_remote_copy(
                src_ref=src(peer),
                dst_ref=dst,
                send_sem=send_sem.at[way],
                recv_sem=recv_sem.at[way, chunk],
                device_id={"seq": peer},
                device_id_type=pl.DeviceIdType.MESH,
            ).start()
            return 0

        lax.fori_loop(1, seq, one, 0)

    def turn(x, way, chunk):
        for j in range(chunk * CHUNK, (chunk + 1) * CHUNK):
            send_in[way, j] = x(j).T.reshape(seq, feats, F2)

    def send_positions(way, chunk):
        part = pl.ds(chunk * CHUNK, CHUNK)
        recv_in[way, me, part] = send_in[way, part, me]
        exchange(
            lambda peer: send_in.at[way, part, peer], recv_in.at[way, me, part], 2 * way, chunk
        )

    def send_features(way, chunk):
        part = pl.ds(chunk * CHUNK, CHUNK)
        recv_out[way, part, me] = send_out[way, me, part]
        exchange(
            lambda peer: send_out.at[way, peer, part], recv_out.at[way, part, me], 2 * way + 1, chunk
        )

    def wait_chunk(way, chunk):
        wait_bytes(
            send_in.at[0, pl.ds(0, CHUNK), pl.ds(0, seq - 1)], recv_sem.at[way, chunk]
        )

    def forward(way, spectrum, spectrum_mid):
        tiles = recv_in[way].reshape(F1 // 2, 2, feats, F2)
        mid = jnp.sum(
            tiles[:, 0].astype(jnp.float32) - tiles[:, 1].astype(jnp.float32), axis=0
        )
        field[...] = recv_in[way].reshape(F1 * feats, F2).astype(jnp.float32)
        cos, sin = twiddle[0], twiddle[1]

        def step(group, _):
            base = group * 4
            halves = []
            for sub in range(2):
                pair = [
                    field[pl.ds(base + 2 * sub + i, F1, stride=feats), :] for i in range(2)
                ]
                two = jnp.concatenate(pair, axis=1).astype(jnp.bfloat16)
                both = dot(whole(outer_fwd), two)
                for i in range(2):
                    real = both[:LINES, i * F2 : (i + 1) * F2]
                    imag = both[LINES:, i * F2 : (i + 1) * F2]
                    halves.append(
                        jnp.concatenate(
                            [real * cos + imag * sin, imag * cos - real * sin], axis=1
                        ).astype(jnp.bfloat16)
                    )
            where = pl.ds(pl.multiple_of(base * LINES, 4 * LINES), 4 * LINES)
            spectrum[where, :] = dot(jnp.concatenate(halves, axis=0), whole(inner_fwd)).astype(
                jnp.bfloat16
            )
            return 0

        lax.fori_loop(0, feats // 4, step, 0)
        cos_mid, sin_mid = twiddle_mid[0], twiddle_mid[1]
        half = jnp.concatenate([mid * cos_mid, -mid * sin_mid], axis=1).astype(jnp.bfloat16)
        spectrum_mid[...] = dot(half, whole(inner_fwd)).astype(jnp.bfloat16)

    def backward(way, product, product_mid):
        cos, sin = twiddle[0], twiddle[1]

        def step(group, _):
            base = group * 4
            where = pl.ds(pl.multiple_of(base * LINES, 4 * LINES), 4 * LINES)
            half = dot(product(where), whole(inner_inv))
            for sub in range(2):
                columns = []
                for i in range(2):
                    part = half[(2 * sub + i) * LINES : (2 * sub + i + 1) * LINES]
                    real, imag = part[:, :F2], part[:, F2:]
                    columns.append(
                        jnp.concatenate(
                            [real * cos - imag * sin, imag * cos + real * sin], axis=0
                        ).astype(jnp.bfloat16)
                    )
                result = dot(whole(outer_inv), jnp.concatenate(columns, axis=1)) * inv_length
                for i in range(2):
                    field[pl.ds(base + 2 * sub + i, F1, stride=feats), :] = result[
                        :, i * F2 : (i + 1) * F2
                    ]
            return 0

        lax.fori_loop(0, feats // 4, step, 0)
        half = dot(product_mid(), whole(inner_inv))
        last = (half[:, :F2] * twiddle_mid[0] - half[:, F2:] * twiddle_mid[1]).astype(jnp.bfloat16)
        last = last.astype(jnp.float32) * inv_length
        both = field[...].reshape(F1 // 2, 2, feats, F2)
        sign = jnp.where(lax.broadcasted_iota(jnp.int32, both.shape, 1) == 0, 1.0, -1.0)
        both = both + sign * last[None, None]
        send_out[way] = both.astype(jnp.bfloat16).reshape(seq, rows, feats, F2)

    def split(z):
        return z[:, :F2].astype(jnp.float32), z[:, F2:].astype(jnp.float32)

    def times(z, f):
        zr, zi = split(z)
        fr, fi = split(f)
        return jnp.concatenate([zr * fr - zi * fi, zr * fi + zi * fr], axis=1).astype(jnp.bfloat16)

    def times_conj(z, f):
        zr, zi = split(z)
        fr, fi = split(f)
        return jnp.concatenate([fr * zr + fi * zi, fr * zi - fi * zr], axis=1)

    loads["filter"].wait()
    scatter_prepare()
    loads["history"].wait()
    for chunk in range(chunks):
        turn(lambda j: history[pl.ds(j * F2, F2), :], 0, chunk)
    pl.semaphore_wait(barrier, 2 * seq - 1 + 5)
    scatter_start()
    for chunk in range(chunks):
        send_positions(0, chunk)
    gather()
    for name in ("outer_fwd", "twiddle", "twiddle_mid", "inner_fwd", "inner_inv", "outer_inv"):
        loads[name].wait()
    for chunk in range(chunks):
        wait_chunk(0, chunk)
    forward(0, spec, spec_mid)
    backward(
        0,
        lambda where: times(spec[where, :], filt[where, :]),
        lambda: times(spec_mid[...], filt_mid[...]),
    )
    for chunk in range(chunks):
        send_features(0, chunk)

    for name in ("gain_first", "bias_first", "w_in", "w_out", "gain_second", "cotangent"):
        loads[name].wait()
    for chunk in range(chunks):
        wait_chunk(1, chunk)
        for j in range(chunk * CHUNK, (chunk + 1) * CHUNK):
            mixed = recv_out[0, j].reshape(seq * feats, F2).T.astype(jnp.float32)
            part = pl.ds(j * F2, F2)
            grad_rows[part, :] = local_rows(
                mixed,
                history[part, :],
                cotangent[part, :],
                gain_first[...],
                bias_first[...],
                w_in[...],
                w_out[...],
                gain_second[...],
            )
        turn(lambda j: grad_rows[pl.ds(j * F2, F2), :].astype(jnp.bfloat16), 1, chunk)
        send_positions(1, chunk)

    for chunk in range(chunks):
        wait_chunk(2, chunk)
    forward(1, back_spec, back_mid)
    reduce_start()
    backward(
        1,
        lambda where: times_conj(back_spec[where, :], filt[where, :]).astype(jnp.bfloat16),
        lambda: times_conj(back_mid[...], filt_mid[...]).astype(jnp.bfloat16),
    )
    reduce_x()
    for chunk in range(chunks):
        send_features(1, chunk)
    reduce_x_second()
    reduce_z()
    reduce_z_second()
    return_grad()
    for chunk in range(chunks):
        wait_chunk(3, chunk)
        for j in range(chunk * CHUNK, (chunk + 1) * CHUNK):
            back = recv_out[1, j].reshape(seq * feats, F2).T.astype(jnp.float32)
            part = pl.ds(j * F2, F2)
            out[part, :] = (grad_rows[part, :] + back).astype(jnp.bfloat16)
        part = pl.ds(chunk * CHUNK * F2, CHUNK * F2)
        pltpu.make_async_copy(out.at[part], out_hbm.at[part], store_sem.at[0]).start()
    return_finish()
    store = pltpu.make_async_copy(filter_grad, filter_grad_hbm, store_sem.at[1])
    store.start()

    wait_all_seq(scatter_send, side_send_sem.at[0])
    for way, ref in sizes.items():
        wait_bytes(ref, side_send_sem.at[way])
    wait_all_seq(return_send, side_send_sem.at[19])
    sent = send_in.at[0, :, pl.ds(0, seq - 1)]
    for way in range(4):
        wait_bytes(sent, send_sem.at[way])
    pltpu.make_async_copy(out, out_hbm, store_sem.at[0]).wait()
    store.wait()


def local(history, cotangent, filter_weight, gain_first, bias_first, w_in, w_out, gain_second):
    user_count, row_count, features = history.shape
    seq = lax.axis_size("seq")
    feats = features // seq
    rows = F1 // seq
    bf16, f32 = jnp.bfloat16, jnp.float32
    tables = [jnp.asarray(t) for t in host_tables()]

    batch = lax.axis_size("batch")
    dma = pltpu.SemaphoreType.DMA
    operands = (
        history.reshape(row_count, features),
        cotangent.reshape(row_count, features),
        filter_weight,
        gain_first.reshape(1, features),
        bias_first.reshape(1, features),
        w_in,
        w_out,
        gain_second.reshape(1, features),
        *tables,
    )
    out, filter_grad = pl.pallas_call(
        functools.partial(kernel, seq, batch),
        out_shape=(
            jax.ShapeDtypeStruct((row_count, features), bf16),
            jax.ShapeDtypeStruct(filter_weight.shape, f32),
        ),
        in_specs=[pl.BlockSpec(memory_space=pltpu.HBM)] * len(operands),
        out_specs=(pl.BlockSpec(memory_space=pltpu.HBM),) * 2,
        scratch_shapes=[
            *[pltpu.VMEM(x.shape, x.dtype) for x in operands],
            pltpu.VMEM((row_count, features), bf16),
            pltpu.VMEM(filter_weight.shape, f32),
            pltpu.VMEM((2, rows, seq, feats, F2), bf16),
            pltpu.VMEM((2, seq, rows, feats, F2), bf16),
            pltpu.VMEM((2, seq, rows, feats, F2), bf16),
            pltpu.VMEM((2, rows, seq, feats, F2), bf16),
            pltpu.VMEM((feats * LINES, 2 * F2), bf16),
            pltpu.VMEM((feats, 2 * F2), bf16),
            pltpu.VMEM((feats * LINES, 2 * F2), bf16),
            pltpu.VMEM((feats, 2 * F2), bf16),
            pltpu.VMEM((feats * LINES, 2 * F2), bf16),
            pltpu.VMEM((feats, 2 * F2), bf16),
            pltpu.VMEM((F1 * feats, F2), f32),
            pltpu.VMEM((2 * LINES * feats, F2), f32),
            pltpu.VMEM((row_count, features), f32),
            pltpu.VMEM((8, 16, 128), f32),
            pltpu.VMEM((seq, 8, 128), f32),
            pltpu.VMEM((seq, 8, 128), f32),
            pltpu.VMEM((ZS, XS, CORES, 5, 16, 128), bf16),
            pltpu.VMEM((ZS, XS, CORES, 5, 16, 128), bf16),
            pltpu.VMEM((ZS, XS, 5, 16, 128), bf16),
            pltpu.VMEM((XS, ZS, 5, 16, 128), bf16),
            pltpu.VMEM((2, 2, 5, 16, 128), bf16),
            pltpu.VMEM((2, ZS, 5, 16, 128), bf16),
            pltpu.VMEM((ZS, 5, 16, 128), bf16),
            pltpu.VMEM((3, 16, 128), bf16),
            pltpu.VMEM((2, 16, 128), bf16),
            pltpu.VMEM((2, 5, 16, 128), bf16),
            pltpu.VMEM((seq, 8, 128), f32),
            pltpu.VMEM((seq, 8, 128), f32),
            dma((len(operands),)),
            dma((2,)),
            dma((4,)),
            dma((4, rows // CHUNK)),
            dma((20,)),
            dma((20,)),
        ],
        compiler_params=pltpu.CompilerParams(
            collective_id=0, has_side_effects=True, vmem_limit_bytes=60 * 2**20
        ),
    )(*operands)
    return (out.reshape(user_count, row_count, features), filter_grad)


def solution(mesh):
    placed = (
        P("batch", "seq", None),
        P("batch", "seq", None),
        P(None, "seq", "batch", None),
        P(),
        P(),
        P(),
        P(),
        P(),
    )
    return jax.shard_map(
        local,
        mesh=mesh,
        in_specs=placed,
        out_specs=(P("batch", "seq", None), P(None, "seq", "batch", None)),
        check_vma=False,
    )
```

time: 118 us -> 115 us (0.975); the launches traced: 117 us -> 112 us
  local copies, waits for them, and re-layouts: 13 us -> 2.53 us
  Pallas kernels: 103 us -> 109 us
    unnamed x34 -> x4, local copies, waits for them, and re-layouts: 13 us -> 2.53 us
    pallas_call x1, Pallas kernels: 103 us -> 109 us  [local(): pl.pallas_call(functools.partial(kernel, seq, batch), out_shape=(jax.Shap...]
where the time goes in v3:
time: 115 us; the launch traced here: 112 us
  Pallas kernels  109 us (95%)
  local copies, waits for them, and re-layouts  2.53 us (2%)
    pallas_call x1, Pallas kernels, local(): pl.pallas_call(functools.partial(kernel, seq, batch), out_shape=(jax.Shap...  109 us
    unnamed x4, local copies, waits for them, and re-layouts  2.53 us

profile of v3, /device:TPU:25, one launch (start us, length us, event | category | flops | bytes accessed | tf_op | source)
XLA Modules:
  0.0 112.4 jit_solution(897511947829071282)
XLA Ops:
  0.6 109.2 %shard_map.167 = (bf16[1024,256]{1,0:T(8,128)(2,1)}, f32[2,8,4,256]{3,2,1,0:T(4,128)}) custom-call(bf16[1024,256]{1,0:T(8,128)(2,1)} %bitcast.7, bf16[1024,256]{1,0:T(8,128)(2,1)} %bitcast.8, bf16[2,8,4,256]{3,2,1,0:T(4,128)(2,1)} %filter_weight_hbm.1, f32[1,256]{1,0:T(1,128)} %bitcast.9, f32[1,256]{1,0:T(1,128)} %bitcast.10, bf16[256,512]{1,0:T(8,128)(2,1)} %w_in_hbm.1, ...), custom_call_target="tpu_custom_call" | custom-call | tf_op jit(solution)/shard_map/pallas_call | solution.py:719
  109.8 0.0 copy-start
  109.8 1.9 %copy.20 = bf16[1,1024,256]{2,1,0:T(8,128)(2,1)} copy(bf16[1,1024,256]{2,1,0:T(8,128)(2,1)} %bitcast.6) | data formatting | bytes 1048576
  111.7 0.0 copy-done
  111.7 0.6 copy.21
Async XLA Ops:
  109.8 1.9 %copy-start = (f32[2,8,4,256]{3,2,1,0:T(4,128)S(1)}, f32[2,8,4,256]{3,2,1,0:T(4,128)}, u32[]{:S(2)}) copy-start(f32[2,8,4,256]{3,2,1,0:T(4,128)} %get-tuple-element.9) | copy-start | bytes 196612

commit v4 on v3

--- a/solution.py
+++ b/solution.py
@@ -177,8 +177,6 @@
     x_half,
     x_recv,
     z_send,
-    z_half_left,
-    z_half_right,
     z_recv,
     return_send,
     return_recv,
@@ -204,11 +202,12 @@
         return (z * XS + x) * CORES + c
 
     x_right, x_left, x_far = (lax.rem(along_x + k, XS) for k in (1, XS - 1, 2))
-    z_right, z_left, z_far = (lax.rem(along_z + k, ZS) for k in (1, ZS - 1, 2))
     to_x_right = {"batch": batch_index(along_z, x_right, core)}
     to_x_left = {"batch": batch_index(along_z, x_left, core)}
-    to_z_right = {"batch": batch_index(z_right, along_x, core)}
-    to_z_left = {"batch": batch_index(z_left, along_x, core)}
+    x_peers = [lax.rem(along_x + k, XS) for k in range(1, XS)]
+    z_peers = [lax.rem(along_z + k, ZS) for k in range(1, ZS)]
+    to_x = [{"batch": batch_index(along_z, x, core)} for x in x_peers]
+    to_z = [{"batch": batch_index(z, along_x, core)} for z in z_peers]
     to_core = {"batch": batch_index(along_z, along_x, 1 - core)}
 
     loads = {}
@@ -249,7 +248,7 @@
         return 0
 
     lax.fori_loop(0, seq, greet_opposite, 0)
-    for peer in (to_x_right, to_x_left, to_z_right, to_z_left, to_core):
+    for peer in (*to_z, *to_x, to_core):
         greet(peer)
     lax.fori_loop(1, seq, greet_seq, 0)
 
@@ -275,26 +274,18 @@
         def _():
             wait_bytes(ref, sem)
 
-    piece = gathered.at[0, 0, 0]
     sizes = {
-        1: piece,
-        2: piece,
-        3: piece.at[pl.ds(0, 3)],
-        4: piece.at[pl.ds(0, 2)],
-        5: gathered.at[:, 0, 0],
-        6: gathered.at[:, 0, 0],
-        7: gathered.at[pl.ds(0, 2), 0, 0],
-        8: gathered.at[pl.ds(0, 2), 0, 0],
+        1: gathered.at[0, 0, 0],
+        2: gathered.at[0, 0, 0],
+        3: gathered.at[0, 0, 0],
+        4: gathered.at[:, pl.ds(0, XS - 1), 0],
         9: gathered.at[:, :, 0],
         10: core_recv,
         11: x_half.at[0],
         12: x_half.at[0],
         13: x_recv.at[0],
         14: x_recv.at[0],
-        15: z_half_left,
-        16: z_half_right,
-        17: z_recv.at[0],
-        18: z_recv.at[0],
+        15: z_recv,
     }
 
     def arrived(*ways):
@@ -332,7 +323,7 @@
 
         lax.fori_loop(jnp.where(low, 1, 0), seq, one, 0)
 
-    def gather():
+    def gather_start():
         wait_all_seq(scatter_recv, side_recv_sem.at[0])
         lane = lax.broadcasted_iota(jnp.int32, (8, 128), 1)
         zeros = jnp.zeros((8, 128), jnp.float32)
@@ -350,27 +341,25 @@
                 jnp.bfloat16
             )
         own = gathered.at[along_z, along_x, core]
-        side_copy(own, own, 1, to_z_right)
-        side_copy(own, own, 2, to_z_left)
-        arrived(1)
-        block = gathered.at[z_left, along_x, core, pl.ds(0, 3)]
-        side_copy(block, block, 3, to_z_right)
-        arrived(2)
-        block = gathered.at[z_right, along_x, core, pl.ds(3, 2)]
-        side_copy(block, block, 4, to_z_left)
-        arrived(3, 4)
-        block = gathered.at[:, along_x, core]
-        side_copy(block, block, 5, to_x_right)
-        side_copy(block, block, 6, to_x_left)
-        arrived(5)
-        block = gathered.at[pl.ds(0, 2), x_left, core]
-        side_copy(block, block, 7, to_x_right)
-        arrived(6)
-        block = gathered.at[pl.ds(2, 2), x_right, core]
-        side_copy(block, block, 8, to_x_left)
-        arrived(7, 8)
+        for k, peer in enumerate(to_z):
+            side_copy(own, own, 1 + k, peer)
+        gather_forward(along_z)
+
+    def gather_forward(z):
+        for peer in to_x:
+            block = gathered.at[z, along_x, core]
+            side_copy(block, block, 4, peer)
+
+    def gather_z(k):
+        arrived(1 + k)
+        gather_forward(lax.rem(along_z + ZS - 1 - k, ZS))
+
+    def gather_core():
+        arrived(4)
         block = gathered.at[:, :, core]
         side_copy(block, block, 9, to_core)
+
+    def gather_finish():
         arrived(9)
         loads["spread"].wait()
         parts = [gathered[:, :, :, t].reshape(batch * 16, 128) for t in range(5)]
@@ -442,21 +431,14 @@
         arrived(13, 14)
         total = x_send[along_x].astype(jnp.float32) + x_recv[0].astype(jnp.float32)
         z_send[...] = (total + x_recv[1].astype(jnp.float32)).astype(jnp.bfloat16)
-        side_copy(z_send.at[z_far, pl.ds(0, 3)], z_half_left, 15, to_z_right)
-        side_copy(z_send.at[z_far, pl.ds(3, 2)], z_half_right, 16, to_z_left)
-
-    def reduce_z_second():
+        for k, peer in enumerate(to_z):
+            side_copy(z_send.at[z_peers[k]], z_recv.at[k], 15, peer)
+
+    def return_grad():
         arrived(15)
-        z_send[z_right, 0:3] = add(z_send[z_right, 0:3], z_half_left[...])
-        side_copy(z_send.at[z_right], z_recv.at[0], 17, to_z_right)
-        arrived(16)
-        z_send[z_left, 3:5] = add(z_send[z_left, 3:5], z_half_right[...])
-        side_copy(z_send.at[z_left], z_recv.at[1], 18, to_z_left)
-
-    def return_grad():
-        arrived(17, 18)
-        total = z_send[along_z].astype(jnp.float32) + z_recv[0].astype(jnp.float32)
-        total = total + z_recv[1].astype(jnp.float32)
+        total = z_send[along_z].astype(jnp.float32)
+        for k in range(ZS - 1):
+            total = total + z_recv[k].astype(jnp.float32)
         tiles = [total[t, :8] for t in range(4)] + [total[t, 8:] for t in range(4)]
         tiles.append(total[4, :8])
         lane = lax.broadcasted_iota(jnp.int32, (8, 128), 1)
@@ -562,7 +544,7 @@
             )
             return 0
 
-        lax.fori_loop(0, feats // 4, step, 0)
+        lax.fori_loop(0, feats // 4, step, 0, unroll=True)
         cos_mid, sin_mid = twiddle_mid[0], twiddle_mid[1]
         half = jnp.concatenate([mid * cos_mid, -mid * sin_mid], axis=1).astype(jnp.bfloat16)
         spectrum_mid[...] = dot(half, whole(inner_fwd)).astype(jnp.bfloat16)
@@ -591,7 +573,7 @@
                     ]
             return 0
 
-        lax.fori_loop(0, feats // 4, step, 0)
+        lax.fori_loop(0, feats // 4, step, 0, unroll=True)
         half = dot(product_mid(), whole(inner_inv))
         last = (half[:, :F2] * twiddle_mid[0] - half[:, F2:] * twiddle_mid[1]).astype(jnp.bfloat16)
         last = last.astype(jnp.float32) * inv_length
@@ -618,16 +600,23 @@
     loads["history"].wait()
     for chunk in range(chunks):
         turn(lambda j: history[pl.ds(j * F2, F2), :], 0, chunk)
-    pl.semaphore_wait(barrier, 2 * seq - 1 + 5)
+    pl.semaphore_wait(barrier, 2 * seq - 1 + ZS - 1 + XS - 1 + 1)
     scatter_start()
-    for chunk in range(chunks):
+    for chunk in range(chunks // 2):
         send_positions(0, chunk)
-    gather()
+    gather_start()
+    gather_z(0)
+    gather_z(2)
+    for chunk in range(chunks // 2, chunks):
+        send_positions(0, chunk)
+    gather_z(1)
     for name in ("outer_fwd", "twiddle", "twiddle_mid", "inner_fwd", "inner_inv", "outer_inv"):
         loads[name].wait()
     for chunk in range(chunks):
         wait_chunk(0, chunk)
     forward(0, spec, spec_mid)
+    gather_core()
+    gather_finish()
     backward(
         0,
         lambda where: times(spec[where, :], filt[where, :]),
@@ -660,17 +649,18 @@
         wait_chunk(2, chunk)
     forward(1, back_spec, back_mid)
     reduce_start()
+    reduce_x()
     backward(
         1,
         lambda where: times_conj(back_spec[where, :], filt[where, :]).astype(jnp.bfloat16),
         lambda: times_conj(back_mid[...], filt_mid[...]).astype(jnp.bfloat16),
     )
-    reduce_x()
-    for chunk in range(chunks):
+    reduce_x_second()
+    for chunk in range(chunks // 2):
         send_features(1, chunk)
-    reduce_x_second()
     reduce_z()
-    reduce_z_second()
+    for chunk in range(chunks // 2, chunks):
+        send_features(1, chunk)
     return_grad()
     for chunk in range(chunks):
         wait_chunk(3, chunk)
@@ -751,9 +741,7 @@
             pltpu.VMEM((2, 2, 5, 16, 128), bf16),
             pltpu.VMEM((2, ZS, 5, 16, 128), bf16),
             pltpu.VMEM((ZS, 5, 16, 128), bf16),
-            pltpu.VMEM((3, 16, 128), bf16),
-            pltpu.VMEM((2, 16, 128), bf16),
-            pltpu.VMEM((2, 5, 16, 128), bf16),
+            pltpu.VMEM((ZS - 1, 5, 16, 128), bf16),
             pltpu.VMEM((seq, 8, 128), f32),
             pltpu.VMEM((seq, 8, 128), f32),
             dma((len(operands),)),

time: 115 us -> 102 us (0.89); the launches traced: 112 us -> 102 us
  Pallas kernels: 109 us -> 99.1 us
    pallas_call x1, Pallas kernels: 109 us -> 99.1 us  [local(): pl.pallas_call(functools.partial(kernel, seq, batch), out_shape=(jax.Shap...]
where the time goes in v4:
time: 102 us
  Pallas kernels  99.1 us (97%)
  local copies, waits for them, and re-layouts  2.53 us (2%)
    pallas_call x1, Pallas kernels, local(): pl.pallas_call(functools.partial(kernel, seq, batch), out_shape=(jax.Shap...  99.1 us
    unnamed x4, local copies, waits for them, and re-layouts  2.53 us

profile of v4, /device:TPU:25, one launch (start us, length us, event | category | flops | bytes accessed | tf_op | source)
XLA Modules:
  0.0 102.3 jit_solution(13568284621680086184)
XLA Ops:
  0.6 99.1 %shard_map.167 = (bf16[1024,256]{1,0:T(8,128)(2,1)}, f32[2,8,4,256]{3,2,1,0:T(4,128)}) custom-call(bf16[1024,256]{1,0:T(8,128)(2,1)} %bitcast.7, bf16[1024,256]{1,0:T(8,128)(2,1)} %bitcast.8, bf16[2,8,4,256]{3,2,1,0:T(4,128)(2,1)} %filter_weight_hbm.1, f32[1,256]{1,0:T(1,128)} %bitcast.9, f32[1,256]{1,0:T(1,128)} %bitcast.10, bf16[256,512]{1,0:T(8,128)(2,1)} %w_in_hbm.1, ...), custom_call_target="tpu_custom_call" | custom-call | tf_op jit(solution)/shard_map/pallas_call | solution.py:709
  99.8 0.0 copy-start
  99.8 1.9 %copy.20 = bf16[1,1024,256]{2,1,0:T(8,128)(2,1)} copy(bf16[1,1024,256]{2,1,0:T(8,128)(2,1)} %bitcast.6) | data formatting | bytes 1048576
  101.7 0.0 copy-done
  101.7 0.6 copy.21
Async XLA Ops:
  99.8 1.9 %copy-start = (f32[2,8,4,256]{3,2,1,0:T(4,128)S(1)}, f32[2,8,4,256]{3,2,1,0:T(4,128)}, u32[]{:S(2)}) copy-start(f32[2,8,4,256]{3,2,1,0:T(4,128)} %get-tuple-element.9) | copy-start | bytes 196612

commit v5 on v4

--- a/solution.py
+++ b/solution.py
@@ -174,7 +174,6 @@
     core_send,
     core_recv,
     x_send,
-    x_half,
     x_recv,
     z_send,
     z_recv,
@@ -201,9 +200,6 @@
     def batch_index(z, x, c):
         return (z * XS + x) * CORES + c
 
-    x_right, x_left, x_far = (lax.rem(along_x + k, XS) for k in (1, XS - 1, 2))
-    to_x_right = {"batch": batch_index(along_z, x_right, core)}
-    to_x_left = {"batch": batch_index(along_z, x_left, core)}
     x_peers = [lax.rem(along_x + k, XS) for k in range(1, XS)]
     z_peers = [lax.rem(along_z + k, ZS) for k in range(1, ZS)]
     to_x = [{"batch": batch_index(along_z, x, core)} for x in x_peers]
@@ -281,8 +277,8 @@
         4: gathered.at[:, pl.ds(0, XS - 1), 0],
         9: gathered.at[:, :, 0],
         10: core_recv,
-        11: x_half.at[0],
-        12: x_half.at[0],
+        11: x_recv.at[0],
+        12: x_recv.at[0],
         13: x_recv.at[0],
         14: x_recv.at[0],
         15: z_recv,
@@ -369,16 +365,18 @@
                 [spread[k, 2 * F2 * h : 2 * F2 * (h + 1)] for k in range(4)], axis=1
             )
             result = dot(table, block).astype(jnp.bfloat16).T.astype(jnp.float32)
-            field[512 * h : 512 * (h + 1), :] = result[:, :F2]
-            field[1024 + 512 * h : 1024 + 512 * (h + 1), :] = result[:, F2:]
+            filt[512 * h : 512 * (h + 1), :] = result[:, :F2]
+            filt[1024 + 512 * h : 1024 + 512 * (h + 1), :] = result[:, F2:]
         table = jnp.concatenate([spread[k, : 2 * F2] for k in range(4)], axis=1)
         filt_mid[...] = dot(table, parts[4]).astype(jnp.bfloat16).T[:feats]
-        for d in range(feats):
-            real = field[pl.ds(d, LINES, stride=feats), :]
-            imag = field[pl.ds(1024 + d, LINES, stride=feats), :]
-            filt[d * LINES : (d + 1) * LINES, :] = jnp.concatenate([real, imag], axis=1).astype(
-                jnp.bfloat16
-            )
+
+    def filter_lines(base):
+        blocks = []
+        for i in range(4):
+            real = filt[pl.ds(base + i, LINES, stride=feats), :]
+            imag = filt[pl.ds(1024 + base + i, LINES, stride=feats), :]
+            blocks.append(jnp.concatenate([real, imag], axis=1))
+        return jnp.concatenate(blocks, axis=0)
 
     def reduce_start():
         for d in range(feats):
@@ -412,27 +410,30 @@
     def add(a, b):
         return (a.astype(jnp.float32) + b.astype(jnp.float32)).astype(jnp.bfloat16)
 
+    z_order = [lax.rem(along_z + k, ZS) for k in (2, 1, 3, 0)]
+
     def reduce_x():
         arrived(10)
-        for x in range(XS):
-            x_send[x] = add(core_send[:, x, core], core_recv[:, x])
-        side_copy(x_send.at[x_far, pl.ds(0, 2)], x_half.at[0], 11, to_x_right)
-        side_copy(x_send.at[x_far, pl.ds(2, 2)], x_half.at[1], 12, to_x_left)
-
-    def reduce_x_second():
-        arrived(11)
-        x_send[x_right, 0:2] = add(x_send[x_right, 0:2], x_half[0])
-        side_copy(x_send.at[x_right], x_recv.at[0], 13, to_x_right)
-        arrived(12)
-        x_send[x_left, 2:4] = add(x_send[x_left, 2:4], x_half[1])
-        side_copy(x_send.at[x_left], x_recv.at[1], 14, to_x_left)
+        for place, z in enumerate(z_order):
+            for x in range(XS):
+                x_send[z, x] = add(core_send[z, x, core], core_recv[z, x])
+            for k, peer in enumerate(to_x):
+                side_copy(x_send.at[z, x_peers[k]], x_recv.at[z, k], 11 + place, peer)
 
     def reduce_z():
-        arrived(13, 14)
-        total = x_send[along_x].astype(jnp.float32) + x_recv[0].astype(jnp.float32)
-        z_send[...] = (total + x_recv[1].astype(jnp.float32)).astype(jnp.bfloat16)
-        for k, peer in enumerate(to_z):
-            side_copy(z_send.at[z_peers[k]], z_recv.at[k], 15, peer)
+        for place, z in enumerate(z_order):
+            arrived(11 + place)
+            total = x_send[z, along_x].astype(jnp.float32)
+            for k in range(XS - 1):
+                total = total + x_recv[z, k].astype(jnp.float32)
+            z_send[z] = total.astype(jnp.bfloat16)
+            if place < ZS - 1:
+                side_copy(
+                    z_send.at[z],
+                    z_recv.at[place],
+                    15,
+                    {"batch": batch_index(z, along_x, core)},
+                )
 
     def return_grad():
         arrived(15)
@@ -447,19 +448,28 @@
             return_send[t] = tiles[t]
             return_send[seq - 1 - t] = jnp.where(lane < 112, moved[t], moved[t + 1])
 
-        def one(k, _):
-            peer = lax.rem(me + k, seq)
-            target = jnp.where(peer < seq // 2, mine, opposite)
+        def send(peer, target):
             side_copy(
                 return_send.at[peer], return_recv.at[me], 19, {"seq": peer, "batch": target}
             )
+
+        half = seq // 2
+
+        def far(k, _):
+            send(half + lax.rem(me + k, half), opposite)
             return 0
+
+        def near(k, _):
+            send(lax.rem(me + k, half), mine)
+            return 0
+
+        lax.fori_loop(0, half, far, 0)
 
         @pl.when(low)
         def _():
             return_recv[me] = return_send[me]
 
-        lax.fori_loop(jnp.where(low, 1, 0), seq, one, 0)
+        lax.fori_loop(jnp.where(low, 1, 0), half, near, 0)
 
     def return_finish():
         wait_all_seq(return_recv, side_recv_sem.at[19])
@@ -513,12 +523,17 @@
             send_in.at[0, pl.ds(0, CHUNK), pl.ds(0, seq - 1)], recv_sem.at[way, chunk]
         )
 
-    def forward(way, spectrum, spectrum_mid):
-        tiles = recv_in[way].reshape(F1 // 2, 2, feats, F2)
-        mid = jnp.sum(
-            tiles[:, 0].astype(jnp.float32) - tiles[:, 1].astype(jnp.float32), axis=0
-        )
-        field[...] = recv_in[way].reshape(F1 * feats, F2).astype(jnp.float32)
+    def absorb(way, chunk):
+        mid = 0.0
+        for source in range(seq):
+            block = recv_in[way, source, chunk * CHUNK : (chunk + 1) * CHUNK].astype(jnp.float32)
+            first = (source * rows + chunk * CHUNK) * feats
+            field[first : first + CHUNK * feats, :] = block.reshape(CHUNK * feats, F2)
+            for j in range(CHUNK):
+                mid = mid + block[j] if j % 2 == 0 else mid - block[j]
+        return mid
+
+    def forward(mid, spectrum, spectrum_mid):
         cos, sin = twiddle[0], twiddle[1]
 
         def step(group, _):
@@ -555,7 +570,7 @@
         def step(group, _):
             base = group * 4
             where = pl.ds(pl.multiple_of(base * LINES, 4 * LINES), 4 * LINES)
-            half = dot(product(where), whole(inner_inv))
+            half = dot(product(where, filter_lines(base)), whole(inner_inv))
             for sub in range(2):
                 columns = []
                 for i in range(2):
@@ -612,14 +627,16 @@
     gather_z(1)
     for name in ("outer_fwd", "twiddle", "twiddle_mid", "inner_fwd", "inner_inv", "outer_inv"):
         loads[name].wait()
+    mid = 0.0
     for chunk in range(chunks):
         wait_chunk(0, chunk)
-    forward(0, spec, spec_mid)
+        mid = mid + absorb(0, chunk)
+    forward(mid, spec, spec_mid)
     gather_core()
     gather_finish()
     backward(
         0,
-        lambda where: times(spec[where, :], filt[where, :]),
+        lambda where, lines: times(spec[where, :], lines),
         lambda: times(spec_mid[...], filt_mid[...]),
     )
     for chunk in range(chunks):
@@ -645,23 +662,24 @@
         turn(lambda j: grad_rows[pl.ds(j * F2, F2), :].astype(jnp.bfloat16), 1, chunk)
         send_positions(1, chunk)
 
+    mid = 0.0
     for chunk in range(chunks):
         wait_chunk(2, chunk)
-    forward(1, back_spec, back_mid)
+        mid = mid + absorb(1, chunk)
+    forward(mid, back_spec, back_mid)
     reduce_start()
     reduce_x()
     backward(
         1,
-        lambda where: times_conj(back_spec[where, :], filt[where, :]).astype(jnp.bfloat16),
+        lambda where, lines: times_conj(back_spec[where, :], lines).astype(jnp.bfloat16),
         lambda: times_conj(back_mid[...], filt_mid[...]).astype(jnp.bfloat16),
     )
-    reduce_x_second()
     for chunk in range(chunks // 2):
         send_features(1, chunk)
     reduce_z()
+    return_grad()
     for chunk in range(chunks // 2, chunks):
         send_features(1, chunk)
-    return_grad()
     for chunk in range(chunks):
         wait_chunk(3, chunk)
         for j in range(chunk * CHUNK, (chunk + 1) * CHUNK):
@@ -726,7 +744,7 @@
             pltpu.VMEM((feats, 2 * F2), bf16),
             pltpu.VMEM((feats * LINES, 2 * F2), bf16),
             pltpu.VMEM((feats, 2 * F2), bf16),
-            pltpu.VMEM((feats * LINES, 2 * F2), bf16),
+            pltpu.VMEM((2 * LINES * feats, F2), f32),
             pltpu.VMEM((feats, 2 * F2), bf16),
             pltpu.VMEM((F1 * feats, F2), f32),
             pltpu.VMEM((2 * LINES * feats, F2), f32),
@@ -737,9 +755,8 @@
             pltpu.VMEM((ZS, XS, CORES, 5, 16, 128), bf16),
             pltpu.VMEM((ZS, XS, CORES, 5, 16, 128), bf16),
             pltpu.VMEM((ZS, XS, 5, 16, 128), bf16),
-            pltpu.VMEM((XS, ZS, 5, 16, 128), bf16),
-            pltpu.VMEM((2, 2, 5, 16, 128), bf16),
-            pltpu.VMEM((2, ZS, 5, 16, 128), bf16),
+            pltpu.VMEM((ZS, XS, 5, 16, 128), bf16),
+            pltpu.VMEM((ZS, XS - 1, 5, 16, 128), bf16),
             pltpu.VMEM((ZS, 5, 16, 128), bf16),
             pltpu.VMEM((ZS - 1, 5, 16, 128), bf16),
             pltpu.VMEM((seq, 8, 128), f32),

time: 102 us -> 99.2 us (0.973)
  Pallas kernels: 99.1 us -> 95.4 us
    pallas_call x1, Pallas kernels: 99.1 us -> 95.4 us  [local(): pl.pallas_call(functools.partial(kernel, seq, batch), out_shape=(jax.Shap...]
where the time goes in v5:
time: 99.2 us; the launch traced here: 98.6 us
  Pallas kernels  95.4 us (96%)
  local copies, waits for them, and re-layouts  2.53 us (3%)
    pallas_call x1, Pallas kernels, local(): pl.pallas_call(functools.partial(kernel, seq, batch), out_shape=(jax.Shap...  95.4 us
    unnamed x4, local copies, waits for them, and re-layouts  2.53 us

profile of v5, /device:TPU:25, one launch (start us, length us, event | category | flops | bytes accessed | tf_op | source)
XLA Modules:
  0.0 98.6 jit_solution(12321956479334873931)
XLA Ops:
  0.6 95.4 %shard_map.167 = (bf16[1024,256]{1,0:T(8,128)(2,1)}, f32[2,8,4,256]{3,2,1,0:T(4,128)}) custom-call(bf16[1024,256]{1,0:T(8,128)(2,1)} %bitcast.7, bf16[1024,256]{1,0:T(8,128)(2,1)} %bitcast.8, bf16[2,8,4,256]{3,2,1,0:T(4,128)(2,1)} %filter_weight_hbm.1, f32[1,256]{1,0:T(1,128)} %bitcast.9, f32[1,256]{1,0:T(1,128)} %bitcast.10, bf16[256,512]{1,0:T(8,128)(2,1)} %w_in_hbm.1, ...), custom_call_target="tpu_custom_call" | custom-call | tf_op jit(solution)/shard_map/pallas_call | solution.py:727
  96.1 0.0 copy-start
  96.1 1.9 %copy.20 = bf16[1,1024,256]{2,1,0:T(8,128)(2,1)} copy(bf16[1,1024,256]{2,1,0:T(8,128)(2,1)} %bitcast.6) | data formatting | bytes 1048576
  98.0 0.0 copy-done
  98.0 0.6 copy.21
Async XLA Ops:
  96.1 1.9 %copy-start = (f32[2,8,4,256]{3,2,1,0:T(4,128)S(1)}, f32[2,8,4,256]{3,2,1,0:T(4,128)}, u32[]{:S(2)}) copy-start(f32[2,8,4,256]{3,2,1,0:T(4,128)} %get-tuple-element.9) | copy-start | bytes 196612

commit v6 on v5

--- a/solution.py
+++ b/solution.py
@@ -53,7 +53,9 @@
         for q in range(F2):
             for h in range(2):
                 spread[h, part * F2 + q, (q // 4) * 16 + h * 8 + part * 4 + q % 4] = 1.0
-            collect[(q // 4) * 8 + part * 4 + q % 4, part * F2 + q] = 1.0
+            block = q // 4
+            place = (block % CORES) * (F2 // 4 // CORES) + block // CORES
+            collect[place * 8 + part * 4 + q % 4, part * F2 + q] = 1.0
     return columns(spread.reshape(4 * F2, 4 * F2)), columns(collect)
 
 
@@ -385,12 +387,11 @@
             grad_field[pl.ds(d, LINES, stride=feats), :] = term[:, :F2]
             grad_field[pl.ds(1024 + d, LINES, stride=feats), :] = term[:, F2:]
         loads["collect"].wait()
-        parts = []
+        operands = []
         for h in range(2):
             real = grad_field[512 * h : 512 * (h + 1), :]
             imag = grad_field[1024 + 512 * h : 1024 + 512 * (h + 1), :]
-            both = jnp.concatenate([real, imag], axis=1).astype(jnp.bfloat16)
-            parts.append(dot_nt(whole(collect), both).reshape(batch, 8, 512))
+            operands.append(jnp.concatenate([real, imag], axis=1).astype(jnp.bfloat16))
         mid = jnp.concatenate(
             [
                 times_conj(back_mid[...], spec_mid[...]) * inv_length,
@@ -398,14 +399,19 @@
             ],
             axis=0,
         ).astype(jnp.bfloat16)
-        last = dot_nt(whole(collect), mid).reshape(batch, 8, 128)
-        both = jnp.concatenate(parts, axis=1).astype(jnp.bfloat16)
-        both = both.reshape(ZS, XS, CORES, 16, 512)
-        for t in range(4):
-            core_send[:, :, :, t] = both[..., 128 * t : 128 * (t + 1)]
-        last = jnp.concatenate([last, jnp.zeros_like(last)], axis=1).astype(jnp.bfloat16)
-        core_send[:, :, :, 4] = last.reshape(ZS, XS, CORES, 16, 128)
-        side_copy(core_send.at[:, :, 1 - core], core_recv, 10, to_core)
+        for c in (1 - core, core):
+            where = pl.ds(pl.multiple_of(c * F2, F2), F2)
+            table = jnp.concatenate([collect[0, where], collect[1, where]], axis=1)
+            parts = [dot_nt(table, x).reshape(batch // CORES, 8, 512) for x in operands]
+            last = dot_nt(table, mid).reshape(batch // CORES, 8, 128)
+            both = jnp.concatenate(parts, axis=1).astype(jnp.bfloat16)
+            both = both.reshape(ZS, XS, 16, 512)
+            for t in range(4):
+                core_send[c, :, :, t] = both[..., 128 * t : 128 * (t + 1)]
+            last = jnp.concatenate([last, jnp.zeros_like(last)], axis=1).astype(jnp.bfloat16)
+            core_send[c, :, :, 4] = last.reshape(ZS, XS, 16, 128)
+            if c is not core:
+                side_copy(core_send.at[c], core_recv, 10, to_core)
 
     def add(a, b):
         return (a.astype(jnp.float32) + b.astype(jnp.float32)).astype(jnp.bfloat16)
@@ -416,7 +422,7 @@
         arrived(10)
         for place, z in enumerate(z_order):
             for x in range(XS):
-                x_send[z, x] = add(core_send[z, x, core], core_recv[z, x])
+                x_send[z, x] = add(core_send[core, z, x], core_recv[z, x])
             for k, peer in enumerate(to_x):
                 side_copy(x_send.at[z, x_peers[k]], x_recv.at[z, k], 11 + place, peer)
 
@@ -674,11 +680,11 @@
         lambda where, lines: times_conj(back_spec[where, :], lines).astype(jnp.bfloat16),
         lambda: times_conj(back_mid[...], filt_mid[...]).astype(jnp.bfloat16),
     )
-    for chunk in range(chunks // 2):
-        send_features(1, chunk)
+    send_features(1, 0)
     reduce_z()
+    send_features(1, 1)
     return_grad()
-    for chunk in range(chunks // 2, chunks):
+    for chunk in range(2, chunks):
         send_features(1, chunk)
     for chunk in range(chunks):
         wait_chunk(3, chunk)
@@ -753,7 +759,7 @@
             pltpu.VMEM((seq, 8, 128), f32),
             pltpu.VMEM((seq, 8, 128), f32),
             pltpu.VMEM((ZS, XS, CORES, 5, 16, 128), bf16),
-            pltpu.VMEM((ZS, XS, CORES, 5, 16, 128), bf16),
+            pltpu.VMEM((CORES, ZS, XS, 5, 16, 128), bf16),
             pltpu.VMEM((ZS, XS, 5, 16, 128), bf16),
             pltpu.VMEM((ZS, XS, 5, 16, 128), bf16),
             pltpu.VMEM((ZS, XS - 1, 5, 16, 128), bf16),

time: 99.2 us -> 96.8 us (0.976); the launches traced: 98.6 us -> 95.2 us
  Pallas kernels: 95.4 us -> 92 us
    pallas_call x1, Pallas kernels: 95.4 us -> 92 us  [local(): pl.pallas_call(functools.partial(kernel, seq, batch), out_shape=(jax.Shap...]
where the time goes in v6:
time: 96.8 us; the launch traced here: 95.2 us
  Pallas kernels  92 us (95%)
  local copies, waits for them, and re-layouts  2.53 us (3%)
    pallas_call x1, Pallas kernels, local(): pl.pallas_call(functools.partial(kernel, seq, batch), out_shape=(jax.Shap...  92 us
    unnamed x4, local copies, waits for them, and re-layouts  2.53 us

profile of v6, /device:TPU:25, one launch (start us, length us, event | category | flops | bytes accessed | tf_op | source)
XLA Modules:
  0.0 95.2 jit_solution(15615864037932033468)
XLA Ops:
  0.6 92.0 %shard_map.167 = (bf16[1024,256]{1,0:T(8,128)(2,1)}, f32[2,8,4,256]{3,2,1,0:T(4,128)}) custom-call(bf16[1024,256]{1,0:T(8,128)(2,1)} %bitcast.7, bf16[1024,256]{1,0:T(8,128)(2,1)} %bitcast.8, bf16[2,8,4,256]{3,2,1,0:T(4,128)(2,1)} %filter_weight_hbm.1, f32[1,256]{1,0:T(1,128)} %bitcast.9, f32[1,256]{1,0:T(1,128)} %bitcast.10, bf16[256,512]{1,0:T(8,128)(2,1)} %w_in_hbm.1, ...), custom_call_target="tpu_custom_call" | custom-call | tf_op jit(solution)/shard_map/pallas_call | solution.py:733
  92.7 0.0 copy-start
  92.7 1.9 %copy.20 = bf16[1,1024,256]{2,1,0:T(8,128)(2,1)} copy(bf16[1,1024,256]{2,1,0:T(8,128)(2,1)} %bitcast.6) | data formatting | bytes 1048576
  94.6 0.0 copy-done
  94.6 0.6 copy.21
Async XLA Ops:
  92.7 1.9 %copy-start = (f32[2,8,4,256]{3,2,1,0:T(4,128)S(1)}, f32[2,8,4,256]{3,2,1,0:T(4,128)}, u32[]{:S(2)}) copy-start(f32[2,8,4,256]{3,2,1,0:T(4,128)} %get-tuple-element.9) | copy-start | bytes 196612

commit v7 on v6

--- a/solution.py
+++ b/solution.py
@@ -598,7 +598,7 @@
         half = dot(product_mid(), whole(inner_inv))
         last = (half[:, :F2] * twiddle_mid[0] - half[:, F2:] * twiddle_mid[1]).astype(jnp.bfloat16)
         last = last.astype(jnp.float32) * inv_length
-        both = field[...].reshape(F1 // 2, 2, feats, F2)
+        both = field[: F1 * feats, :].reshape(F1 // 2, 2, feats, F2)
         sign = jnp.where(lax.broadcasted_iota(jnp.int32, both.shape, 1) == 0, 1.0, -1.0)
         both = both + sign * last[None, None]
         send_out[way] = both.astype(jnp.bfloat16).reshape(seq, rows, feats, F2)
@@ -750,10 +750,10 @@
             pltpu.VMEM((feats, 2 * F2), bf16),
             pltpu.VMEM((feats * LINES, 2 * F2), bf16),
             pltpu.VMEM((feats, 2 * F2), bf16),
-            pltpu.VMEM((2 * LINES * feats, F2), f32),
+            pltpu.VMEM((2 * LINES * feats + feats, F2), f32),
             pltpu.VMEM((feats, 2 * F2), bf16),
-            pltpu.VMEM((F1 * feats, F2), f32),
-            pltpu.VMEM((2 * LINES * feats, F2), f32),
+            pltpu.VMEM((F1 * feats + feats, F2), f32),
+            pltpu.VMEM((2 * LINES * feats + feats, F2), f32),
             pltpu.VMEM((row_count, features), f32),
             pltpu.VMEM((8, 16, 128), f32),
             pltpu.VMEM((seq, 8, 128), f32),

time: 96.8 us -> 96.7 us (level)
  no operation moved by 1% of the time
where the time goes in v7:
time: 96.7 us; the launch traced here: 95.2 us
  Pallas kernels  92 us (95%)
  local copies, waits for them, and re-layouts  2.53 us (3%)
    pallas_call x1, Pallas kernels, local(): pl.pallas_call(functools.partial(kernel, seq, batch), out_shape=(jax.Shap...  92 us
    unnamed x4, local copies, waits for them, and re-layouts  2.53 us

profile of v7, /device:TPU:25, one launch (start us, length us, event | category | flops | bytes accessed | tf_op | source)
XLA Modules:
  0.0 95.2 jit_solution(15951868756468093200)
XLA Ops:
  0.6 92.0 %shard_map.167 = (bf16[1024,256]{1,0:T(8,128)(2,1)}, f32[2,8,4,256]{3,2,1,0:T(4,128)}) custom-call(bf16[1024,256]{1,0:T(8,128)(2,1)} %bitcast.7, bf16[1024,256]{1,0:T(8,128)(2,1)} %bitcast.8, bf16[2,8,4,256]{3,2,1,0:T(4,128)(2,1)} %filter_weight_hbm.1, f32[1,256]{1,0:T(1,128)} %bitcast.9, f32[1,256]{1,0:T(1,128)} %bitcast.10, bf16[256,512]{1,0:T(8,128)(2,1)} %w_in_hbm.1, ...), custom_call_target="tpu_custom_call" | custom-call | tf_op jit(solution)/shard_map/pallas_call | solution.py:733
  92.7 0.0 copy-start
  92.7 1.9 %copy.20 = bf16[1,1024,256]{2,1,0:T(8,128)(2,1)} copy(bf16[1,1024,256]{2,1,0:T(8,128)(2,1)} %bitcast.6) | data formatting | bytes 1048576
  94.6 0.0 copy-done
  94.6 0.6 copy.21
Async XLA Ops:
  92.7 1.9 %copy-start = (f32[2,8,4,256]{3,2,1,0:T(4,128)S(1)}, f32[2,8,4,256]{3,2,1,0:T(4,128)}, u32[]{:S(2)}) copy-start(f32[2,8,4,256]{3,2,1,0:T(4,128)} %get-tuple-element.9) | copy-start | bytes 196612
